TPU v7x, 256 devices: a whole 4x4x8 slice. The times are simulated.
256 devices in a mesh: section: 32 (over z_hi, y, core), dp: 8 (over z_lo, x).
Axes of the slice: x: 4, y: 4, z: 8 (z_hi: 4, z_lo: 2; z = z_hi * 2 + z_lo), core: 2. Of those that a mesh axis runs over, the one named last changes fastest.
Arguments:
- activations: bfloat16 [32, 64, 64, 4096], P('section', 'dp'), may hold values from -6 to 6
- out_grads: bfloat16 [32, 64, 64, 4096], P('section', 'dp'), may hold values from -6 to 6
- proj_in: bfloat16 [32, 2, 4096, 128], P('section'), may hold values from -0.09375 to 0.09375
- proj_out: bfloat16 [32, 2, 64, 4096], P('section'), may hold values from -0.09375 to 0.09375
- earlier_gram: float32 [8192, 8192], P('section', 'dp'), may hold values from -4 to 4, as said below
Outputs:
- gram: float32 [8192, 8192], P('section', 'dp')
Inputs may be any that keep to these rules, and one draw needn't show every extreme that they name: earlier_gram is symmetric.
All inputs are finite; a program needn't handle non-finite values.
Results may differ from a plain program's by a relative error of at most 0.0013.
Values sent between devices are 32-bit elements; how exact they have to be, the bound alone decides.
No kernel may reach another device: no remote copies, remote signals or barrier semaphores. Data moves between devices by JAX's collectives and lax.ppermute only.
A program may use at most 64 MiB of HBM per device.

v0:
```python
import math

import jax
import jax.numpy as jnp
from jax import lax
from jax.sharding import PartitionSpec as P

PROJ = 2
LEN = 64


def per_device(activations, out_grads, proj_in, proj_out, earlier_gram):
    layer_act = activations[0]
    layer_grad = out_grads[0]
    layer_in = proj_in[0]
    layer_out = proj_out[0]
    low_in = jnp.einsum(
        "etd,pdm->petm", layer_act, layer_in, preferred_element_type=jnp.float32
    ).astype(jnp.bfloat16)
    low_out = jnp.einsum(
        "pkd,etd->pekt", layer_out, layer_grad, preferred_element_type=jnp.float32
    ).astype(jnp.bfloat16)
    partial_terms = jnp.einsum(
        "pekt,petm->ekm", low_out, low_in, preferred_element_type=jnp.float32
    )
    local_count = partial_terms.shape[0]
    partial_terms = partial_terms.reshape(local_count, -1)
    n_layers = lax.axis_size("section")
    n_groups = lax.axis_size("dp")
    total_examples = local_count * n_groups
    scale = 1.0 / math.sqrt(LEN * n_layers * PROJ)
    row_width = earlier_gram.shape[0]
    col_width = earlier_gram.shape[1]
    row_start = lax.axis_index("section") * row_width
    col_start = lax.axis_index("dp") * col_width
    placed = jnp.zeros((total_examples, partial_terms.shape[1]), jnp.float32)
    placed = lax.dynamic_update_slice_in_dim(
        placed, partial_terms, lax.axis_index("dp") * local_count, 0
    )
    features = lax.psum(placed, ("section", "dp")) * scale
    row_block = lax.dynamic_slice_in_dim(features, row_start, row_width, 1)
    col_block = lax.dynamic_slice_in_dim(features, col_start, col_width, 1)
    outer = jnp.dot(row_block.T, col_block, precision=lax.Precision.HIGHEST)
    return earlier_gram + outer / total_examples


def solution(mesh):
    return jax.shard_map(
        per_device,
        mesh=mesh,
        in_specs=(
            P("section", "dp", None, None),
            P("section", "dp", None, None),
            P("section", None, None, None),
            P("section", None, None, None),
            P("section", "dp"),
        ),
        out_specs=P("section", "dp"),
        check_vma=False,
    )
```

profile of v0, /device:TPU:1, one launch (start us, length us, event | category | flops | bytes accessed | tf_op | source)
XLA Modules:
  0.0 291.7 jit_solution(597952820103288470)
XLA Ops:
  6.5 0.0 copy-start
  6.5 0.0 all-reduce.2.cloned.1.call-start
  6.5 4.8 %fusion.14 = bf16[2,8,64,64]{3,2,0,1:T(8,128)(2,1)S(1)} fusion(bf16[1,8,64,4096]{3,2,1,0:T(8,128)(2,1)} %param.6, bf16[1,2,64,4096]{3,2,1,0:T(8,128)(2,1)} %param.8), kind=kOutput, calls=%fused_computation.9 | convolution fusion | flops 536936448 | bytes 5373952 | tf_op jit(solution)/shard_map/pkd,etd->pekt/dot_general | solution.py:20
  11.3 0.0 copy-done
  11.3 3.6 %convolution_bitcast_fusion = f32[1,8,64,128]{3,2,1,0:T(8,128)S(1)} fusion(bf16[2,8,64,64]{3,2,0,1:T(8,128)(2,1)S(1)} %fusion.14, bf16[1,8,64,4096]{3,2,1,0:T(8,128)(2,1)} %param.5, bf16[1,2,4096,128]{3,2,1,0:T(8,128)(2,1)S(1)} %copy-done), kind=kOutput, calls=%fused_computation.10 | convolution fusion | flops 1090650112 | bytes 6684672 | tf_op jit(solution)/shard_map/pekt,petm->ekm/dot_general | solution.py:23
  15.0 1.5 broadcast_in_dim.3
  16.5 0.9 bitcast_dynamic-update-slice_fusion
  17.3 0.0 all-reduce.2.cloned.1.call-update
  17.4 0.0 copy-start.1
  17.4 263.7 %all-reduce.2.cloned.1.call-done = f32[64,8192]{1,0:T(8,128)} async-done(((f32[64,8192]{1,0:T(8,128)}), f32[64,8192]{1,0:T(8,128)}) %all-reduce.2.cloned.1.call-update) | async-done | bytes 2097168 | tf_op jit(solution)/shard_map/psum | solution.py:40
  281.0 1.8 broadcast_multiply_fusion
  282.8 0.0 copy-done.1
  282.8 2.0 fusion.5
Async XLA Ops:
  6.5 4.8 %copy-start = (bf16[1,2,4096,128]{3,2,1,0:T(8,128)(2,1)S(1)}, bf16[1,2,4096,128]{3,2,1,0:T(8,128)(2,1)}, u32[]{:S(2)}) copy-start(bf16[1,2,4096,128]{3,2,1,0:T(8,128)(2,1)} %param.7) | copy-start | bytes 6291460
  6.5 274.5 %all-reduce.2.cloned.1.call-start = ((), (), s32[]{:S(2)}) async-start(), calls=%async_computation | async-start | bytes 4194304 | tf_op jit(solution)/shard_map/psum | solution.py:40
  17.4 265.4 %copy-start.1 = (f32[256,1024]{1,0:T(8,128)S(1)}, f32[256,1024]{1,0:T(8,128)}, u32[]{:S(2)}) copy-start(f32[256,1024]{1,0:T(8,128)} %param.9) | copy-start | bytes 3145732
Sparse Core Ops, SparseCore 0:
  17.5 263.5 all-reduce.1
where the time goes:
time: 293 us; the launch traced here: 292 us
  waiting for transfers between devices  264 us (90%)
  between operations  13.4 us (5%)
  matrix products  10.4 us (4%)
    psum x1, waiting for transfers between devices, per_device(): features = lax.psum(placed, ('section', 'dp')) * scale  264 us
  transfers between devices with their start and end apart: 1, of which 1 were waited for; matrix products, arithmetic and copies ran while one was open for 0% of the time, Pallas kernels for 0%

commit v1 on v0

v1 whole, which is shorter than its diff:
```python
import jax
import jax.numpy as jnp
from jax import lax
from jax.sharding import PartitionSpec as P

PROJ = 2
LEN = 64
BOTH = ("section", "dp")
ZH, Y, C, ZL, X = 4, 4, 2, 2, 4
SECTIONS, GROUPS = ZH * Y * C, ZL * X
PAIRS = SECTIONS // C


def device_at(zh, y, c, zl, x):
    return ((zh * Y + y) * C + c) * GROUPS + zl * X + x


def first_half(y, d):
    t = (y - 2 * (d % 2)) % 4
    return (t == 1) | (t == 2)


def column_routes(turn):
    pairs = []
    for zh in range(ZH):
        for y in range(Y):
            for zl in range(ZL):
                for x in range(X):
                    d = zl * X + x
                    from_zh = d // 2
                    t = (y - 2 * (d % 2)) % 4
                    half = int(first_half(y, d)) ^ turn
                    from_y = 2 * (d % 2) + half
                    from_x = (x + 2 - (zh - from_zh)) % X
                    from_zl = zl if t >= 2 else 1 - zl
                    for c in range(C):
                        pairs.append(
                            (
                                device_at(from_zh, from_y, c, from_zl, from_x),
                                device_at(zh, y, c, zl, x),
                            )
                        )
    return pairs


ACROSS_CORES = [(s, s ^ 1) for s in range(SECTIONS)]
SAME_CORE = [[p * C + c for p in range(PAIRS)] for c in range(C)]


def per_device(activations, out_grads, proj_in, proj_out, earlier_gram):
    section = lax.axis_index("section")
    dp = lax.axis_index("dp")
    core = section % C
    y = (section // C) % Y
    low_in = jnp.einsum(
        "etd,pdm->petm", activations[0], proj_in[0], preferred_element_type=jnp.float32
    ).astype(jnp.bfloat16)
    low_out = jnp.einsum(
        "pkd,etd->pekt", proj_out[0], out_grads[0], preferred_element_type=jnp.float32
    ).astype(jnp.bfloat16)
    terms = jnp.einsum(
        "pekt,petm->ekm", low_out, low_in, preferred_element_type=jnp.float32
    )
    count = terms.shape[0]
    half = count // C
    terms = terms.reshape(count, -1)
    width = terms.shape[1]
    pair_width = width // PAIRS
    row_width = earlier_gram.shape[0]

    theirs = lax.dynamic_slice_in_dim(terms, (1 - core) * half, half, 0)
    mine = lax.dynamic_slice_in_dim(terms, core * half, half, 0)
    mine = mine + lax.ppermute(theirs, "section", ACROSS_CORES)
    pieces = mine.reshape(half, PAIRS, pair_width).transpose(1, 0, 2)
    pieces = lax.all_to_all(pieces, "section", 0, 0, axis_index_groups=SAME_CORE)
    reduced = pieces.sum(0)
    rows = lax.all_to_all(
        jnp.broadcast_to(reduced, (GROUPS, half, pair_width)), "dp", 0, 0
    )
    rows = rows.reshape(GROUPS * half, pair_width)
    row_mine = lax.dynamic_slice_in_dim(rows, core * row_width, row_width, 1)
    row_theirs = lax.dynamic_slice_in_dim(rows, (1 - core) * row_width, row_width, 1)
    row_other = lax.ppermute(row_theirs, "section", ACROSS_CORES)
    got = [lax.ppermute(rows, BOTH, column_routes(turn)) for turn in range(2)]
    swap = first_half(y, dp)
    cols = jnp.concatenate(
        [jnp.where(swap, got[1], got[0]), jnp.where(swap, got[0], got[1])], 1
    )
    cols_other = lax.ppermute(cols, "section", ACROSS_CORES)
    row_block = jnp.concatenate([row_mine, row_other], 0)
    col_block = jnp.concatenate([cols, cols_other], 0)
    outer = jnp.dot(row_block.T, col_block, precision=lax.Precision.HIGHEST)
    total_examples = count * GROUPS
    return earlier_gram + outer * (1.0 / (LEN * SECTIONS * PROJ * total_examples))


def solution(mesh):
    return jax.shard_map(
        per_device,
        mesh=mesh,
        in_specs=(
            P("section", "dp", None, None),
            P("section", "dp", None, None),
            P("section", None, None, None),
            P("section", None, None, None),
            P("section", "dp"),
        ),
        out_specs=P("section", "dp"),
        check_vma=False,
    )
```

time: 293 us -> 60.8 us (0.21)
  the two profiles are of different devices: /device:TPU:1 before, /device:TPU:39 now
where the time goes in v1:
time: 60.8 us; the launch traced here: 60.6 us
  blocking collectives  26.6 us (44%)
  waiting for transfers between devices  12.1 us (20%)
  matrix products  11.2 us (18%)
  starting transfers between devices  8.67 us (14%)
  local copies, waits for them, and re-layouts  1.84 us (3%)
    all_to_all x1, blocking collectives, per_device(): lax.all_to_all(pieces, 'section', 0, 0, axis_index_groups=SAME_CORE)  19 us
    ppermute x2, waiting for transfers between devices, per_device(): got = [lax.ppermute(rows, BOTH, column_routes(turn)) for turn in range(2)]  9.81 us
    all_to_all x1, blocking collectives, per_device(): lax.all_to_all(jnp.broadcast_to(reduced, (GROUPS, half, pair_width)), 'dp...  7.6 us
    dot_general x1, matrix products, per_device(): jnp.einsum('pkd,etd->pekt', proj_out[0], out_grads[0], preferred_element_...  4.8 us
    ppermute x2, starting transfers between devices, per_device(): got = [lax.ppermute(rows, BOTH, column_routes(turn)) for turn in range(2)]  4.44 us
    dot_general x1, matrix products, per_device(): jnp.einsum('pekt,petm->ekm', low_out, low_in, preferred_element_type=jnp....  4.42 us
    ppermute x1, starting transfers between devices, per_device(): cols_other = lax.ppermute(cols, 'section', ACROSS_CORES)  3.45 us
    dot_general x1, matrix products, per_device(): outer = jnp.dot(row_block.T, col_block, precision=lax.Precision.HIGHEST)  2.01 us
  transfers between devices with their start and end apart: 5, of which 4 were waited for; matrix products, arithmetic and copies ran while one was open for 0% of the time, Pallas kernels for 0%

profile of v1, /device:TPU:39, one launch (start us, length us, event | category | flops | bytes accessed | tf_op | source)
XLA Modules:
  0.0 60.6 jit_solution(6466606779389893149)
XLA Ops:
  0.0 0.0 copy-start
  0.0 4.8 %fusion.14 = bf16[2,8,64,64]{3,2,0,1:T(8,128)(2,1)S(1)} fusion(bf16[1,8,64,4096]{3,2,1,0:T(8,128)(2,1)} %param.6, bf16[1,2,64,4096]{3,2,1,0:T(8,128)(2,1)} %param.8), kind=kOutput, calls=%fused_computation.9 | convolution fusion | flops 536936448 | bytes 5373952 | tf_op jit(solution)/shard_map/pkd,etd->pekt/dot_general | solution.py:58
  4.8 0.0 copy-done
  4.8 0.0 copy-start.1
  4.8 4.4 %convolution_bitcast_fusion = f32[1,8,64,128]{3,2,1,0:T(8,128)} fusion(bf16[2,8,64,64]{3,2,0,1:T(8,128)(2,1)S(1)} %fusion.14, bf16[1,8,64,4096]{3,2,1,0:T(8,128)(2,1)} %param.5, bf16[1,2,4096,128]{3,2,1,0:T(8,128)(2,1)S(1)} %copy-done), kind=kOutput, calls=%fused_computation.10 | convolution fusion | flops 1090650112 | bytes 6684672 | tf_op jit(solution)/shard_map/pekt,petm->ekm/dot_general | solution.py:61
  9.3 1.1 %copy.11 = f32[1,8,64,128]{3,1,2,0:T(8,128)S(1)} copy(f32[1,8,64,128]{3,2,1,0:T(8,128)} %convolution_bitcast_fusion) | data formatting | bytes 524288
  10.4 0.7 %constant_dynamic-slice_fusion.2 = f32[4,8192]{1,0:T(4,128)} fusion(f32[8,8192]{1,0:T(8,128)S(1)} %bitcast.53, s32[]{:T(128)S(6)} %select_n.49), kind=kLoop, calls=%fused_computation.28 | loop fusion | bytes 262148 | tf_op jit(solution)/shard_map/dynamic_slice | solution.py:71
  11.1 0.7 %collective-permute-start = (f32[4,8192]{1,0:T(4,128)}, f32[4,8192]{1,0:T(4,128)S(1)}, u32[]{:S(2)}, u32[]{:S(2)}) collective-permute-start(f32[4,8192]{1,0:T(4,128)} %constant_dynamic-slice_fusion.2), channel_id=1, source_target_pairs={{0,8},{8,0},{16,24},{24,16},{32,40},{40,32},{48,56},{56,48},{64,72... | collective-permute-start | bytes 393224 | tf_op jit(solution)/shard_map/ppermute | solution.py:73
  11.7 1.2 %collective-permute-done = f32[4,8192]{1,0:T(4,128)S(1)} collective-permute-done((f32[4,8192]{1,0:T(4,128)}, f32[4,8192]{1,0:T(4,128)S(1)}, u32[]{:S(2)}, u32[]{:S(2)}) %collective-permute-start) | collective-permute-done | bytes 131104 | tf_op jit(solution)/shard_map/ppermute | solution.py:73
  13.0 19.0 %all_to_all.10 = f32[16,4,512]{2,1,0:T(4,128)S(1)} all-to-all(f32[16,4,512]{2,1,0:T(4,128)S(1)} %bitcast.55), channel_id=1, replica_groups={{0,16,32,48,64,80,96,112,128,144,160,176,192,208,224,240},{8,24,40,56,7..., dimensions={0} | all-to-all | bytes 262144 | tf_op jit(solution)/shard_map/all_to_all | solution.py:75
  32.0 7.6 %all_to_all.11 = f32[8,4,512]{2,1,0:T(4,128)S(1)} all-to-all(f32[8,4,512]{2,1,0:T(4,128)S(1)} %broadcast_in_dim.3), channel_id=1, replica_groups=mesh['section'=32,'dp'=8] {'dp'}, dimensions={0} | all-to-all | bytes 131072 | tf_op jit(solution)/shard_map/all_to_all | solution.py:77
  39.6 3.5 %collective-permute-start.2 = (f32[32,512]{1,0:T(8,128)S(1)}, f32[32,512]{1,0:T(8,128)S(1)}, u32[]{:S(2)}, u32[]{:S(2)}) collective-permute-start(f32[32,512]{1,0:T(8,128)S(1)} %reshape.11), channel_id=1, source_target_pairs={{22,0},{30,8},{35,1},{43,9},{85,2},{93,10},{98,3},{106,11},{144,4}... | collective-permute-start | bytes 196616 | tf_op jit(solution)/shard_map/ppermute | solution.py:84
  43.1 1.0 %collective-permute-start.3 = (f32[32,512]{1,0:T(8,128)S(1)}, f32[32,512]{1,0:T(8,128)S(1)}, u32[]{:S(2)}, u32[]{:S(2)}) collective-permute-start(f32[32,512]{1,0:T(8,128)S(1)} %reshape.11), channel_id=1, source_target_pairs={{6,0},{14,8},{51,1},{59,9},{69,2},{77,10},{114,3},{122,11},{128,4}... | collective-permute-start | bytes 196616 | tf_op jit(solution)/shard_map/ppermute | solution.py:84
  44.0 5.9 %collective-permute-done.2 = f32[32,512]{1,0:T(8,128)S(1)} collective-permute-done((f32[32,512]{1,0:T(8,128)S(1)}, f32[32,512]{1,0:T(8,128)S(1)}, u32[]{:S(2)}, u32[]{:S(2)}) %collective-permute-start.2) | collective-permute-done | bytes 65568 | tf_op jit(solution)/shard_map/ppermute | solution.py:84
  50.0 3.9 %collective-permute-done.3 = f32[32,512]{1,0:T(8,128)S(1)} collective-permute-done((f32[32,512]{1,0:T(8,128)S(1)}, f32[32,512]{1,0:T(8,128)S(1)}, u32[]{:S(2)}, u32[]{:S(2)}) %collective-permute-start.3) | collective-permute-done | bytes 65568 | tf_op jit(solution)/shard_map/ppermute | solution.py:84
  53.9 3.5 %collective-permute-start.4 = (f32[32,1024]{1,0:T(8,128)S(1)}, f32[32,1024]{1,0:T(8,128)S(1)}, u32[]{:S(2)}, u32[]{:S(2)}) collective-permute-start(f32[32,1024]{1,0:T(8,128)S(1)} %pad_maximum_fusion), channel_id=1, source_target_pairs={{0,8},{8,0},{16,24},{24,16},{32,40},{40,32},{48,56},{56,48},{64,72... | collective-permute-start | bytes 393224 | tf_op jit(solution)/shard_map/ppermute | solution.py:89
  57.4 0.1 collective-permute-start.1
  57.5 1.1 %collective-permute-done.1 = f32[32,256]{1,0:T(8,128)S(1)} collective-permute-done((f32[32,256]{1,0:T(8,128)S(1)}, f32[32,256]{1,0:T(8,128)S(1)}, u32[]{:S(2)}, u32[]{:S(2)}) %collective-permute-start.1) | collective-permute-done | bytes 32800 | tf_op jit(solution)/shard_map/ppermute | solution.py:83
  58.6 0.0 collective-permute-done.4
  58.6 0.0 copy-done.1
  58.6 2.0 %fusion.5 = f32[256,1024]{1,0:T(8,128)} fusion(f32[256,1024]{1,0:T(8,128)S(1)} %copy-done.1, f32[32,1024]{1,0:T(8,128)S(1)} %collective-permute-done.4, f32[32,512]{1,0:T(8,128)S(1)} %get-tuple-element.6, f32[32,512]{1,0:T(8,128)S(1)} %get-tuple-element.5, f32[32,256]{1,0:T(8,128)S(1)} %collective-permute-done.1, f32[32,256]{1,0:T(8,128)S(1)} %get-tuple-element.7), kind=kOutput, calls=%fused_computation.6 | convolution fusion | flops 201998336 | bytes 2424832 | tf_op jit(solution)/shard_map/dot_general | solution.py:92
  (7 shorter events, 0.1 us)
Async XLA Ops:
  0.0 4.8 %copy-start = (bf16[1,2,4096,128]{3,2,1,0:T(8,128)(2,1)S(1)}, bf16[1,2,4096,128]{3,2,1,0:T(8,128)(2,1)}, u32[]{:S(2)}) copy-start(bf16[1,2,4096,128]{3,2,1,0:T(8,128)(2,1)} %param.7) | copy-start | bytes 6291460
  4.8 53.7 %copy-start.1 = (f32[256,1024]{1,0:T(8,128)S(1)}, f32[256,1024]{1,0:T(8,128)}, u32[]{:S(2)}) copy-start(f32[256,1024]{1,0:T(8,128)} %param.9) | copy-start | bytes 3145732
  11.1 1.9 %collective-permute-start = (f32[4,8192]{1,0:T(4,128)}, f32[4,8192]{1,0:T(4,128)S(1)}, u32[]{:S(2)}, u32[]{:S(2)}) collective-permute-start(f32[4,8192]{1,0:T(4,128)} %constant_dynamic-slice_fusion.2), channel_id=1, source_target_pairs={{0,8},{8,0},{16,24},{24,16},{32,40},{40,32},{48,56},{56,48},{64,72... | collective-permute-start | bytes 393224 | tf_op jit(solution)/shard_map/ppermute | solution.py:73
  39.6 10.4 %collective-permute-start.2 = (f32[32,512]{1,0:T(8,128)S(1)}, f32[32,512]{1,0:T(8,128)S(1)}, u32[]{:S(2)}, u32[]{:S(2)}) collective-permute-start(f32[32,512]{1,0:T(8,128)S(1)} %reshape.11), channel_id=1, source_target_pairs={{22,0},{30,8},{35,1},{43,9},{85,2},{93,10},{98,3},{106,11},{144,4}... | collective-permute-start | bytes 196616 | tf_op jit(solution)/shard_map/ppermute | solution.py:84
  43.1 10.8 %collective-permute-start.3 = (f32[32,512]{1,0:T(8,128)S(1)}, f32[32,512]{1,0:T(8,128)S(1)}, u32[]{:S(2)}, u32[]{:S(2)}) collective-permute-start(f32[32,512]{1,0:T(8,128)S(1)} %reshape.11), channel_id=1, source_target_pairs={{6,0},{14,8},{51,1},{59,9},{69,2},{77,10},{114,3},{122,11},{128,4}... | collective-permute-start | bytes 196616 | tf_op jit(solution)/shard_map/ppermute | solution.py:84
  53.9 4.7 %collective-permute-start.4 = (f32[32,1024]{1,0:T(8,128)S(1)}, f32[32,1024]{1,0:T(8,128)S(1)}, u32[]{:S(2)}, u32[]{:S(2)}) collective-permute-start(f32[32,1024]{1,0:T(8,128)S(1)} %pad_maximum_fusion), channel_id=1, source_target_pairs={{0,8},{8,0},{16,24},{24,16},{32,40},{40,32},{48,56},{56,48},{64,72... | collective-permute-start | bytes 393224 | tf_op jit(solution)/shard_map/ppermute | solution.py:89
  57.4 1.2 %collective-permute-start.1 = (f32[32,256]{1,0:T(8,128)S(1)}, f32[32,256]{1,0:T(8,128)S(1)}, u32[]{:S(2)}, u32[]{:S(2)}) collective-permute-start(f32[32,256]{1,0:T(8,128)S(1)} %get-tuple-element.8), channel_id=1, source_target_pairs={{0,8},{8,0},{16,24},{24,16},{32,40},{40,32},{48,56},{56,48},{64,72... | collective-permute-start | bytes 98312 | tf_op jit(solution)/shard_map/ppermute | solution.py:83

commit v2 on v0

v2 whole, which is shorter than its diff:
```python
import functools

import jax
import jax.numpy as jnp
from jax import lax
from jax.experimental import pallas as pl
from jax.experimental.pallas import tpu as pltpu
from jax.sharding import PartitionSpec as P

PROJ = 2
LEN = 64
LANES = 128
BOTH = ("section", "dp")
ZH, Y, C, ZL, X = 4, 4, 2, 2, 4
SECTIONS, GROUPS = ZH * Y * C, ZL * X
PAIRS = SECTIONS // C
CHUNK = 512
VMEM_BYTES = 53 * 2**20
F32 = jnp.float32


def device_at(zh, y, c, zl, x):
    return ((zh * Y + y) * C + c) * GROUPS + zl * X + x


ROUTES = [(10, 0), (34, 1), (67, 2), (99, 3), (137, 4), (161, 5), (204, 6), (239, 7), (25, 8), (58, 9), (83, 10), (122, 11), (148, 12), (189, 13), (215, 14), (242, 15), (14, 16), (43, 17), (66, 18), (107, 19), (136, 20), (165, 21), (199, 22), (228, 23), (26, 24), (56, 25), (88, 26), (123, 27), (157, 28), (185, 29), (223, 30), (255, 31), (2, 32), (32, 33), (74, 34), (104, 35), (128, 36), (166, 37), (198, 38), (229, 39), (30, 40), (57, 41), (91, 42), (115, 43), (152, 44), (177, 45), (221, 46), (254, 47), (11, 48), (42, 49), (73, 50), (96, 51), (140, 52), (173, 53), (207, 54), (236, 55), (24, 56), (59, 57), (90, 58), (113, 59), (144, 60), (184, 61), (222, 62), (245, 63), (5, 64), (38, 65), (75, 66), (98, 67), (139, 68), (162, 69), (205, 70), (235, 71), (21, 72), (55, 73), (82, 74), (120, 75), (146, 76), (187, 77), (210, 78), (247, 79), (6, 80), (44, 81), (64, 82), (105, 83), (130, 84), (168, 85), (194, 86), (231, 87), (17, 88), (52, 89), (80, 90), (114, 91), (154, 92), (176, 93), (214, 94), (243, 95), (8, 96), (39, 97), (72, 98), (106, 99), (133, 100), (170, 101), (202, 102), (238, 103), (22, 104), (63, 105), (81, 106), (121, 107), (153, 108), (179, 109), (219, 110), (251, 111), (15, 112), (47, 113), (65, 114), (97, 115), (138, 116), (171, 117), (206, 118), (227, 119), (29, 120), (62, 121), (89, 122), (112, 123), (147, 124), (186, 125), (218, 126), (252, 127), (13, 128), (37, 129), (69, 130), (102, 131), (142, 132), (160, 133), (203, 134), (230, 135), (31, 136), (54, 137), (92, 138), (125, 139), (155, 140), (190, 141), (209, 142), (241, 143), (7, 144), (36, 145), (76, 146), (109, 147), (129, 148), (163, 149), (192, 150), (224, 151), (23, 152), (61, 153), (84, 154), (126, 155), (158, 156), (191, 157), (208, 158), (250, 159), (4, 160), (46, 161), (77, 162), (108, 163), (135, 164), (175, 165), (197, 166), (232, 167), (28, 168), (53, 169), (93, 170), (117, 171), (145, 172), (180, 173), (211, 174), (248, 175), (12, 176), (45, 177), (68, 178), (101, 179), (131, 180), (167, 181), (195, 182), (225, 183), (20, 184), (60, 185), (87, 186), (116, 187), (159, 188), (183, 189), (217, 190), (240, 191), (9, 192), (33, 193), (71, 194), (103, 195), (134, 196), (174, 197), (200, 198), (237, 199), (19, 200), (50, 201), (86, 202), (127, 203), (151, 204), (188, 205), (220, 206), (249, 207), (1, 208), (40, 209), (70, 210), (111, 211), (141, 212), (164, 213), (193, 214), (226, 215), (18, 216), (49, 217), (95, 218), (119, 219), (150, 220), (181, 221), (213, 222), (244, 223), (0, 224), (35, 225), (78, 226), (110, 227), (132, 228), (169, 229), (196, 230), (234, 231), (27, 232), (48, 233), (85, 234), (118, 235), (149, 236), (182, 237), (216, 238), (253, 239), (3, 240), (41, 241), (79, 242), (100, 243), (143, 244), (172, 245), (201, 246), (233, 247), (16, 248), (51, 249), (94, 250), (124, 251), (156, 252), (178, 253), (212, 254), (246, 255)]


def column_routes():
    return ROUTES


ACROSS_CORES = [(s, s ^ 1) for s in range(SECTIONS)]
SAME_CORE = [[p * C + c for p in range(PAIRS)] for c in range(C)]
SAME_PAIR = [
    [(p * C + c) * GROUPS + d for d in range(GROUPS) for c in range(C)]
    for p in range(PAIRS)
]


def terms_kernel(
    act_ref, grad_ref, in_ref, out_ref, mine_ref, theirs_ref,
    act, grad, weight_in, weight_out, low_in, low_out, sems,
):
    core = lax.rem(lax.axis_index("section"), C)
    count, length, width = act.shape
    tokens = count * length
    half = count // C
    k_out, k_in = out_ref.shape[2], in_ref.shape[3]
    group = k_out // PAIRS
    chunks = width // CHUNK

    def copies(c):
        at = pl.ds(c * CHUNK, CHUNK)
        return [
            pltpu.make_async_copy(in_ref.at[0, :, at, :], weight_in.at[:, at, :], sems.at[c, 0]),
            pltpu.make_async_copy(act_ref.at[0, :, :, at], act.at[:, :, at], sems.at[c, 1]),
            pltpu.make_async_copy(out_ref.at[0, :, :, at], weight_out.at[:, :, at], sems.at[c, 2]),
            pltpu.make_async_copy(grad_ref.at[0, :, :, at], grad.at[:, :, at], sems.at[c, 3]),
        ]

    for c in range(chunks):
        for copy in copies(c):
            copy.start()
    sum_in = sum_out = None
    for c in range(chunks):
        for copy in copies(c):
            copy.wait()
        at = slice(c * CHUNK, (c + 1) * CHUNK)
        part_in = jnp.dot(
            act[:, :, at].reshape(tokens, CHUNK),
            jnp.concatenate([weight_in[p, at, :] for p in range(PROJ)], axis=1),
            preferred_element_type=F32,
        )
        part_out = lax.dot_general(
            grad[:, :, at].reshape(tokens, CHUNK),
            weight_out[:, :, at].reshape(PROJ * k_out, CHUNK),
            (((1,), (1,)), ((), ())),
            preferred_element_type=F32,
        )
        sum_in = part_in if c == 0 else sum_in + part_in
        sum_out = part_out if c == 0 else sum_out + part_out
    low_in[...] = sum_in.astype(jnp.bfloat16)
    low_out[...] = sum_out.astype(jnp.bfloat16)
    for ref, owner in ((theirs_ref, 1 - core), (mine_ref, core)):
        for i in range(half):
            at = pl.ds(pl.multiple_of((owner * half + i) * length, length), length)
            both = lax.dot_general(
                low_out[at, :],
                low_in[at, :],
                (((0,), (0,)), ((), ())),
                preferred_element_type=F32,
            )
            term = both[:k_out, :k_in] + both[k_out:, k_in:]
            for z in range(PAIRS):
                ref[z, i * group : (i + 1) * group, :] = term[z * group : (z + 1) * group]


def layer_terms(activations, out_grads, proj_in, proj_out):
    count, length, width = activations.shape[1:]
    k_in, k_out = proj_in.shape[3], proj_out.shape[2]
    piece = jax.ShapeDtypeStruct((PAIRS, (count // C) * (k_out // PAIRS), k_in), F32)
    return pl.pallas_call(
        terms_kernel,
        in_specs=[pl.BlockSpec(memory_space=pl.ANY)] * 4,
        out_specs=[pl.BlockSpec(memory_space=pltpu.VMEM)] * 2,
        out_shape=[piece, piece],
        scratch_shapes=[
            pltpu.VMEM(activations.shape[1:], jnp.bfloat16),
            pltpu.VMEM(out_grads.shape[1:], jnp.bfloat16),
            pltpu.VMEM(proj_in.shape[1:], jnp.bfloat16),
            pltpu.VMEM(proj_out.shape[1:], jnp.bfloat16),
            pltpu.VMEM((count * length, PROJ * k_in), jnp.bfloat16),
            pltpu.VMEM((count * length, PROJ * k_out), jnp.bfloat16),
            pltpu.SemaphoreType.DMA((width // CHUNK, 4)),
        ],
        compiler_params=pltpu.CompilerParams(vmem_limit_bytes=VMEM_BYTES),
    )(activations, out_grads, proj_in, proj_out)


def gram_kernel(scale, row_ref, near_ref, far_ref, earlier_ref, gram_ref):
    core = lax.rem(lax.axis_index("section"), C)
    per_pair = 4
    examples = row_ref.shape[0] // per_pair
    rows = jnp.concatenate(
        [
            row_ref[pl.ds(core * 2 + i, examples, stride=per_pair), :]
            for i in range(2)
        ],
        axis=1,
    )
    rows = rows * scale
    for ref, owner in ((near_ref, core), (far_ref, 1 - core)):
        cols = jnp.concatenate(
            [ref[pl.ds(k, examples, stride=per_pair), :] for k in range(per_pair)],
            axis=1,
        )
        outer = lax.dot_general(
            rows,
            cols,
            (((0,), (0,)), ((), ())),
            precision=lax.Precision.HIGHEST,
            preferred_element_type=F32,
        )
        width = per_pair * LANES
        at = pl.ds(pl.multiple_of(owner * width, width), width)
        gram_ref[:, at] = earlier_ref[:, at] + outer


def add_gram(scale, rows, near, far, earlier_gram):
    return pl.pallas_call(
        functools.partial(gram_kernel, scale),
        in_specs=[pl.BlockSpec(memory_space=pltpu.VMEM)] * 4,
        out_specs=pl.BlockSpec(memory_space=pltpu.VMEM),
        out_shape=jax.ShapeDtypeStruct(earlier_gram.shape, F32),
        compiler_params=pltpu.CompilerParams(vmem_limit_bytes=16 * 2**20),
    )(rows, near, far, earlier_gram)


def per_device(activations, out_grads, proj_in, proj_out, earlier_gram):
    mine, theirs = layer_terms(activations, out_grads, proj_in, proj_out)
    mine = mine + lax.ppermute(theirs, "section", ACROSS_CORES)
    pieces = lax.all_to_all(mine, "section", 0, 0, axis_index_groups=SAME_CORE)
    reduced = pieces.sum(0)
    rows = lax.all_to_all(
        jnp.broadcast_to(reduced, (GROUPS * C, *reduced.shape)),
        BOTH,
        0,
        0,
        axis_index_groups=SAME_PAIR,
    )
    rows = rows.reshape(-1, LANES)
    near = lax.ppermute(rows, BOTH, column_routes())
    far = lax.ppermute(near, "section", ACROSS_CORES)
    total_examples = activations.shape[1] * GROUPS
    scale = 1.0 / (LEN * SECTIONS * PROJ * total_examples)
    return add_gram(scale, rows, near, far, earlier_gram)


def solution(mesh):
    return jax.shard_map(
        per_device,
        mesh=mesh,
        in_specs=(
            P("section", "dp", None, None),
            P("section", "dp", None, None),
            P("section", None, None, None),
            P("section", None, None, None),
            P("section", "dp"),
        ),
        out_specs=P("section", "dp"),
        check_vma=False,
    )
```

time: 293 us -> 53.8 us (0.18)
  the two profiles are of different devices: /device:TPU:1 before, /device:TPU:35 now
where the time goes in v2:
time: 53.8 us; the launch traced here: 53.7 us
  blocking collectives  30.7 us (57%)
  waiting for transfers between devices  10.3 us (19%)
  Pallas kernels  7.42 us (14%)
  starting transfers between devices  5.17 us (10%)
    all_to_all x1, blocking collectives, per_device(): pieces = lax.all_to_all(mine, 'section', 0, 0, axis_index_groups=SAME_CORE)  19 us
    all_to_all x1, blocking collectives, per_device(): lax.all_to_all(jnp.broadcast_to(reduced, (GROUPS * C, *reduced.shape)), B...  11.7 us
    ppermute x1, waiting for transfers between devices, per_device(): near = lax.ppermute(rows, BOTH, column_routes())  8.37 us
    pallas_call x1, Pallas kernels, layer_terms(): pl.pallas_call(terms_kernel, in_specs=[pl.BlockSpec(memory_space=pl.ANY)]...  5.42 us
    ppermute x1, starting transfers between devices, per_device(): far = lax.ppermute(near, 'section', ACROSS_CORES)  2.58 us
    pallas_call x1, Pallas kernels, add_gram(): pl.pallas_call(functools.partial(gram_kernel, scale), in_specs=[pl.BlockS...  2 us
    ppermute x1, starting transfers between devices, per_device(): near = lax.ppermute(rows, BOTH, column_routes())  1.81 us
  transfers between devices with their start and end apart: 3, of which 3 were waited for; matrix products, arithmetic and copies ran while one was open for 0% of the time, Pallas kernels for 0%

profile of v2, /device:TPU:35, one launch (start us, length us, event | category | flops | bytes accessed | tf_op | source)
XLA Modules:
  0.0 53.7 jit_solution(1308854854148015513)
XLA Ops:
  0.0 0.0 copy-start
  0.0 5.4 %shard_map.55 = (f32[16,16,128]{2,1,0:T(8,128)S(1)}, f32[16,16,128]{2,1,0:T(8,128)S(1)}) custom-call(bf16[1,8,64,4096]{3,2,1,0:T(8,128)(2,1)} %act_ref.1, bf16[1,8,64,4096]{3,2,1,0:T(8,128)(2,1)} %grad_ref.1, bf16[1,2,4096,128]{3,2,1,0:T(8,128)(2,1)} %in_ref.1, bf16[1,2,64,4096]{3,2,1,0:T(8,128)(2,1)} %out_ref.1), custom_call_target="tpu_custom_call" | custom-call | tf_op jit(solution)/shard_map/pallas_call | solution.py:103
  5.4 0.8 %collective-permute-start = (f32[16,16,128]{2,1,0:T(8,128)S(1)}, f32[16,16,128]{2,1,0:T(8,128)S(1)}, u32[]{:S(2)}, u32[]{:S(2)}) collective-permute-start(f32[16,16,128]{2,1,0:T(8,128)S(1)} %get-tuple-element.8), channel_id=1, source_target_pairs={{0,8},{8,0},{16,24},{24,16},{32,40},{40,32},{48,56},{56,48},{64,72... | collective-permute-start | bytes 393224 | tf_op jit(solution)/shard_map/ppermute | solution.py:162
  6.2 1.0 %collective-permute-done = f32[16,16,128]{2,1,0:T(8,128)S(1)} collective-permute-done((f32[16,16,128]{2,1,0:T(8,128)S(1)}, f32[16,16,128]{2,1,0:T(8,128)S(1)}, u32[]{:S(2)}, u32[]{:S(2)}) %collective-permute-start) | collective-permute-done | bytes 131104 | tf_op jit(solution)/shard_map/ppermute | solution.py:162
  7.2 19.0 %all_to_all.10 = f32[16,16,128]{2,1,0:T(8,128)S(1)} all-to-all(f32[16,16,128]{2,1,0:T(8,128)S(1)} %add.3), channel_id=1, replica_groups={{0,16,32,48,64,80,96,112,128,144,160,176,192,208,224,240},{8,24,40,56,7..., dimensions={0} | all-to-all | bytes 262144 | tf_op jit(solution)/shard_map/all_to_all | solution.py:163
  26.2 11.7 %all_to_all.11 = f32[16,16,128]{2,1,0:T(8,128)S(1)} all-to-all(f32[16,16,128]{2,1,0:T(8,128)S(1)} %broadcast_in_dim.3), channel_id=1, replica_groups={{0,8,1,9,2,10,3,11,4,12,5,13,6,14,7,15},{16,24,17,25,18,26,19,27,20,28,..., dimensions={0} | all-to-all | bytes 262144 | tf_op jit(solution)/shard_map/all_to_all | solution.py:165
  37.9 1.8 %collective-permute-start.1 = (f32[256,128]{1,0:T(8,128)S(1)}, f32[256,128]{1,0:T(8,128)S(1)}, u32[]{:S(2)}, u32[]{:S(2)}) collective-permute-start(f32[256,128]{1,0:T(8,128)S(1)} %bitcast.1), channel_id=1, source_target_pairs={{10,0},{34,1},{67,2},{99,3},{137,4},{161,5},{204,6},{239,7},{25,8}... | collective-permute-start | bytes 393224 | tf_op jit(solution)/shard_map/ppermute | solution.py:173
  39.7 8.4 %collective-permute-done.1.near_ref = f32[256,128]{1,0:T(8,128)S(1)} collective-permute-done((f32[256,128]{1,0:T(8,128)S(1)}, f32[256,128]{1,0:T(8,128)S(1)}, u32[]{:S(2)}, u32[]{:S(2)}) %collective-permute-start.1) | collective-permute-done | bytes 131104 | tf_op jit(solution)/shard_map/ppermute | solution.py:173
  48.1 2.6 %collective-permute-start.2 = (f32[256,128]{1,0:T(8,128)S(1)}, f32[256,128]{1,0:T(8,128)S(1)}, u32[]{:S(2)}, u32[]{:S(2)}) collective-permute-start(f32[256,128]{1,0:T(8,128)S(1)} %collective-permute-done.1.near_ref), channel_id=1, source_target_pairs={{0,8},{8,0},{16,24},{24,16},{32,40},{40,32},{48,56},{56,48},{64,72... | collective-permute-start | bytes 393224 | tf_op jit(solution)/shard_map/ppermute | solution.py:174
  50.7 1.0 %collective-permute-done.2.far_ref = f32[256,128]{1,0:T(8,128)S(1)} collective-permute-done((f32[256,128]{1,0:T(8,128)S(1)}, f32[256,128]{1,0:T(8,128)S(1)}, u32[]{:S(2)}, u32[]{:S(2)}) %collective-permute-start.2) | collective-permute-done | bytes 131104 | tf_op jit(solution)/shard_map/ppermute | solution.py:174
  51.7 0.0 copy-done
  51.7 2.0 %shard_map.56 = f32[256,1024]{1,0:T(8,128)} custom-call(f32[256,128]{1,0:T(8,128)S(1)} %bitcast.2, f32[256,128]{1,0:T(8,128)S(1)} %collective-permute-done.1.near_ref, f32[256,128]{1,0:T(8,128)S(1)} %collective-permute-done.2.far_ref, f32[256,1024]{1,0:T(8,128)S(1)} %copy-done), custom_call_target="tpu_custom_call" | custom-call | tf_op jit(solution)/shard_map/pallas_call | solution.py:151
  (3 shorter events, 0.0 us)
Async XLA Ops:
  0.0 51.7 %copy-start = (f32[256,1024]{1,0:T(8,128)S(1)}, f32[256,1024]{1,0:T(8,128)}, u32[]{:S(2)}) copy-start(f32[256,1024]{1,0:T(8,128)} %earlier_ref.1) | copy-start | bytes 3145732
  5.4 1.8 %collective-permute-start = (f32[16,16,128]{2,1,0:T(8,128)S(1)}, f32[16,16,128]{2,1,0:T(8,128)S(1)}, u32[]{:S(2)}, u32[]{:S(2)}) collective-permute-start(f32[16,16,128]{2,1,0:T(8,128)S(1)} %get-tuple-element.8), channel_id=1, source_target_pairs={{0,8},{8,0},{16,24},{24,16},{32,40},{40,32},{48,56},{56,48},{64,72... | collective-permute-start | bytes 393224 | tf_op jit(solution)/shard_map/ppermute | solution.py:162
  37.9 10.2 %collective-permute-start.1 = (f32[256,128]{1,0:T(8,128)S(1)}, f32[256,128]{1,0:T(8,128)S(1)}, u32[]{:S(2)}, u32[]{:S(2)}) collective-permute-start(f32[256,128]{1,0:T(8,128)S(1)} %bitcast.1), channel_id=1, source_target_pairs={{10,0},{34,1},{67,2},{99,3},{137,4},{161,5},{204,6},{239,7},{25,8}... | collective-permute-start | bytes 393224 | tf_op jit(solution)/shard_map/ppermute | solution.py:173
  48.1 3.6 %collective-permute-start.2 = (f32[256,128]{1,0:T(8,128)S(1)}, f32[256,128]{1,0:T(8,128)S(1)}, u32[]{:S(2)}, u32[]{:S(2)}) collective-permute-start(f32[256,128]{1,0:T(8,128)S(1)} %collective-permute-done.1.near_ref), channel_id=1, source_target_pairs={{0,8},{8,0},{16,24},{24,16},{32,40},{40,32},{48,56},{56,48},{64,72... | collective-permute-start | bytes 393224 | tf_op jit(solution)/shard_map/ppermute | solution.py:174

commit v3 on v2

v3 whole, which is shorter than its diff:
```python
import functools

import jax
import jax.numpy as jnp
from jax import lax
from jax.experimental import pallas as pl
from jax.experimental.pallas import tpu as pltpu
from jax.sharding import PartitionSpec as P

PROJ = 2
LEN = 64
LANES = 128
BOTH = ("section", "dp")
ZH, Y, C, ZL, X = 4, 4, 2, 2, 4
SECTIONS, GROUPS = ZH * Y * C, ZL * X
PAIRS = SECTIONS // C
CHUNK = 512
VMEM_BYTES = 53 * 2**20
F32 = jnp.float32


ACROSS_CORES = [(s, s ^ 1) for s in range(SECTIONS)]
def section_at(zh, y, c):
    return (zh * Y + y) * C + c


def shifted(by_zh, by_y):
    return [
        (section_at(zh, y, c), section_at((zh + by_zh) % ZH, (y + by_y) % Y, c))
        for zh in range(ZH)
        for y in range(Y)
        for c in range(C)
    ]


ALONG_ZH = [[section_at(zh, y, c) for zh in range(ZH)] for y in range(Y) for c in range(C)]
SAME_ZH = [
    [section_at(zh, y, c) * GROUPS + d for y in range(Y) for d in range(GROUPS)]
    for zh in range(ZH)
    for c in range(C)
]
SHARE = 3


def terms_kernel(
    act_ref, grad_ref, in_ref, out_ref, mine_ref, theirs_ref,
    act, grad, weight_in, weight_out, low_in, low_out, term, sems,
):
    section = lax.axis_index("section")
    core = lax.rem(section, C)
    y = lax.rem(lax.div(section, C), Y)
    count, length, width = act.shape
    tokens = count * length
    half = count // C
    k_out, k_in = out_ref.shape[2], in_ref.shape[3]
    group = k_out // PAIRS
    chunks = width // CHUNK

    def copies(c):
        at = pl.ds(c * CHUNK, CHUNK)
        return [
            pltpu.make_async_copy(in_ref.at[0, :, at, :], weight_in.at[:, at, :], sems.at[c, 0]),
            pltpu.make_async_copy(act_ref.at[0, :, :, at], act.at[:, :, at], sems.at[c, 1]),
            pltpu.make_async_copy(out_ref.at[0, :, :, at], weight_out.at[:, :, at], sems.at[c, 2]),
            pltpu.make_async_copy(grad_ref.at[0, :, :, at], grad.at[:, :, at], sems.at[c, 3]),
        ]

    for c in range(chunks):
        for copy in copies(c):
            copy.start()
    sum_in = sum_out = None
    for c in range(chunks):
        for copy in copies(c):
            copy.wait()
        at = slice(c * CHUNK, (c + 1) * CHUNK)
        part_in = jnp.dot(
            act[:, :, at].reshape(tokens, CHUNK),
            jnp.concatenate([weight_in[p, at, :] for p in range(PROJ)], axis=1),
            preferred_element_type=F32,
        )
        part_out = lax.dot_general(
            grad[:, :, at].reshape(tokens, CHUNK),
            weight_out[:, :, at].reshape(PROJ * k_out, CHUNK),
            (((1,), (1,)), ((), ())),
            preferred_element_type=F32,
        )
        sum_in = part_in if c == 0 else sum_in + part_in
        sum_out = part_out if c == 0 else sum_out + part_out
    low_in[...] = sum_in.astype(jnp.bfloat16)
    low_out[...] = sum_out.astype(jnp.bfloat16)
    for ref, owner in ((theirs_ref, 1 - core), (mine_ref, core)):
        for i in range(half):
            at = pl.ds(pl.multiple_of((owner * half + i) * length, length), length)
            both = lax.dot_general(
                low_out[at, :],
                low_in[at, :],
                (((0,), (0,)), ((), ())),
                preferred_element_type=F32,
            )
            term[...] = both[:k_out, :k_in] + both[k_out:, k_in:]
            for k in range(group):
                ref[lax.rem(k - y + Y, Y), pl.ds(i, PAIRS, stride=half), :] = term[
                    pl.ds(k, PAIRS, stride=group), :
                ]


def layer_terms(activations, out_grads, proj_in, proj_out):
    count, length, width = activations.shape[1:]
    k_in, k_out = proj_in.shape[3], proj_out.shape[2]
    piece = jax.ShapeDtypeStruct((k_out // PAIRS, PAIRS * (count // C), k_in), F32)
    return pl.pallas_call(
        terms_kernel,
        in_specs=[pl.BlockSpec(memory_space=pl.ANY)] * 4,
        out_specs=[pl.BlockSpec(memory_space=pltpu.VMEM)] * 2,
        out_shape=[piece, piece],
        scratch_shapes=[
            pltpu.VMEM(activations.shape[1:], jnp.bfloat16),
            pltpu.VMEM(out_grads.shape[1:], jnp.bfloat16),
            pltpu.VMEM(proj_in.shape[1:], jnp.bfloat16),
            pltpu.VMEM(proj_out.shape[1:], jnp.bfloat16),
            pltpu.VMEM((count * length, PROJ * k_in), jnp.bfloat16),
            pltpu.VMEM((count * length, PROJ * k_out), jnp.bfloat16),
            pltpu.VMEM((k_out, k_in), F32),
            pltpu.SemaphoreType.DMA((width // CHUNK, 4)),
        ],
        compiler_params=pltpu.CompilerParams(vmem_limit_bytes=VMEM_BYTES),
    )(activations, out_grads, proj_in, proj_out)


def thirds(value):
    parts = []
    for _ in range(3):
        part = value.astype(jnp.bfloat16)
        parts.append(part)
        value = value - part.astype(F32)
    return parts


def pack_kernel(ref_0, ref_1, ref_2, ref_3, packed_ref, reduced):
    zh = lax.div(lax.axis_index("section"), Y * C)
    reduced[...] = (ref_0[...] + ref_1[...]) + (ref_2[...] + ref_3[...])
    half = reduced.shape[0] // PAIRS
    for y in range(Y):
        row = reduced[pl.ds(pl.multiple_of((zh * Y + y) * half, half), half), :]
        for d in range(GROUPS):
            at = (y * GROUPS + d) * SHARE * half
            packed_ref[at : at + half, :] = row
            packed_ref[at + half : at + SHARE * half, :] = reduced[
                d * 2 * half : (d + 1) * 2 * half, :
            ]


def pack(pieces):
    shape = pieces[0].shape
    return pl.pallas_call(
        pack_kernel,
        in_specs=[pl.BlockSpec(memory_space=pltpu.VMEM)] * ZH,
        out_specs=pl.BlockSpec(memory_space=pltpu.VMEM),
        out_shape=jax.ShapeDtypeStruct(
            (Y * GROUPS * SHARE * (shape[0] // PAIRS), shape[1]), F32
        ),
        scratch_shapes=[pltpu.VMEM(shape, F32)],
        compiler_params=pltpu.CompilerParams(vmem_limit_bytes=8 * 2**20),
    )(*pieces)


def gathered(ref, k, row):
    half = ref.shape[0] // (Y * GROUPS * SHARE)
    return jnp.concatenate(
        [
            ref[pl.ds((k * GROUPS * SHARE + row) * half + e, GROUPS, stride=SHARE * half), :]
            for e in range(half)
        ],
        axis=0,
    )


def outer_product(ref, core, scale):
    r = thirds(
        jnp.concatenate([gathered(ref, core * 2 + k, 0) for k in range(2)], axis=1) * scale
    )
    c = thirds(
        jnp.concatenate([gathered(ref, k, 1 + j) for j in range(2) for k in range(4)], axis=1)
    )
    pairs = [(0, 0), (0, 1), (1, 0), (1, 1), (0, 2), (2, 0)]
    return lax.dot_general(
        jnp.concatenate([r[i] for i, _ in pairs], axis=0),
        jnp.concatenate([c[j] for _, j in pairs], axis=0),
        (((0,), (0,)), ((), ())),
        preferred_element_type=F32,
    )


def gram_kernel(scale, ref, earlier_ref, gram_ref):
    core = lax.rem(lax.axis_index("section"), C)
    gram_ref[...] = earlier_ref[...] + outer_product(ref, core, scale)


def add_gram(scale, features, earlier_gram):
    shape = earlier_gram.shape
    return pl.pallas_call(
        functools.partial(gram_kernel, scale),
        in_specs=[pl.BlockSpec(memory_space=pltpu.VMEM)] * 2,
        out_specs=pl.BlockSpec(memory_space=pltpu.VMEM),
        out_shape=jax.ShapeDtypeStruct(shape, F32),
        cost_estimate=pl.CostEstimate(
            flops=12 * shape[0] * shape[1] * 32,
            bytes_accessed=4 * shape[0] * shape[1],
            transcendentals=0,
        ),
        compiler_params=pltpu.CompilerParams(vmem_limit_bytes=16 * 2**20),
    )(features, earlier_gram)


def per_device(activations, out_grads, proj_in, proj_out, earlier_gram):
    mine, theirs = layer_terms(activations, out_grads, proj_in, proj_out)
    mine = mine + lax.ppermute(theirs, "section", ACROSS_CORES)
    reduced = mine[0]
    for turn in (2, 1, 3):
        reduced = reduced + lax.ppermute(mine[turn], "section", shifted(0, turn))
    pieces = [reduced] + [
        lax.ppermute(reduced, "section", shifted(turn, 0)) for turn in (2, 1, 3)
    ]
    packed = pack(pieces)
    rows = packed.shape[0] // (Y * GROUPS * SHARE)
    packed = packed.reshape(Y * GROUPS, SHARE, rows, LANES)
    near = lax.all_to_all(packed, BOTH, 0, 0, axis_index_groups=SAME_ZH)
    near = near.reshape(-1, LANES)
    far = lax.ppermute(near, "section", ACROSS_CORES)
    total_examples = activations.shape[1] * GROUPS
    scale = 1.0 / (LEN * SECTIONS * PROJ * total_examples)
    return add_gram(scale, far, add_gram(scale, near, earlier_gram))


def solution(mesh):
    return jax.shard_map(
        per_device,
        mesh=mesh,
        in_specs=(
            P("section", "dp", None, None),
            P("section", "dp", None, None),
            P("section", None, None, None),
            P("section", None, None, None),
            P("section", "dp"),
        ),
        out_specs=P("section", "dp"),
        check_vma=False,
    )
```

time: 53.8 us -> 48.5 us (0.901)
  the two profiles are of different devices: /device:TPU:35 before, /device:TPU:1 now
where the time goes in v3:
time: 48.5 us; the launch traced here: 48.4 us
  starting transfers between devices  20 us (41%)
  blocking collectives  12.8 us (26%)
  waiting for transfers between devices  8.41 us (17%)
  Pallas kernels  7.12 us (15%)
    all_to_all x1, blocking collectives, per_device(): near = lax.all_to_all(packed, BOTH, 0, 0, axis_index_groups=SAME_ZH)  12.8 us
    ppermute x3, starting transfers between devices, per_device(): lax.ppermute(reduced, 'section', shifted(turn, 0))  9.36 us
    pallas_call x1, Pallas kernels, layer_terms(): pl.pallas_call(terms_kernel, in_specs=[pl.BlockSpec(memory_space=pl.ANY)]...  5.45 us
    ppermute x1, starting transfers between devices, per_device(): far = lax.ppermute(near, 'section', ACROSS_CORES)  4.57 us
    ppermute x3, waiting for transfers between devices, per_device(): lax.ppermute(reduced, 'section', shifted(turn, 0))  3.42 us
    ppermute x1, starting transfers between devices, per_device(): mine = mine + lax.ppermute(theirs, 'section', ACROSS_CORES)  3.35 us
    ppermute x3, waiting for transfers between devices, per_device(): reduced = reduced + lax.ppermute(mine[turn], 'section', shifted(0, turn))  3.28 us
    ppermute x3, starting transfers between devices, per_device(): reduced = reduced + lax.ppermute(mine[turn], 'section', shifted(0, turn))  2.73 us
  transfers between devices with their start and end apart: 8, of which 7 were waited for; matrix products, arithmetic and copies ran while one was open for 0% of the time, Pallas kernels for 1%

profile of v3, /device:TPU:1, one launch (start us, length us, event | category | flops | bytes accessed | tf_op | source)
XLA Modules:
  0.0 48.4 jit_solution(15541225683712290984)
XLA Ops:
  0.0 0.0 copy-start
  0.0 5.4 %shard_map.55 = (f32[4,64,128]{2,1,0:T(8,128)S(1)}, f32[4,64,128]{2,1,0:T(8,128)S(1)}) custom-call(bf16[1,8,64,4096]{3,2,1,0:T(8,128)(2,1)} %act_ref.1, bf16[1,8,64,4096]{3,2,1,0:T(8,128)(2,1)} %grad_ref.1, bf16[1,2,4096,128]{3,2,1,0:T(8,128)(2,1)} %in_ref.1, bf16[1,2,64,4096]{3,2,1,0:T(8,128)(2,1)} %out_ref.1), custom_call_target="tpu_custom_call" | custom-call | tf_op jit(solution)/shard_map/pallas_call | solution.py:111
  5.5 3.3 %collective-permute-start = (f32[4,64,128]{2,1,0:T(8,128)S(1)}, f32[4,64,128]{2,1,0:T(8,128)S(1)}, u32[]{:S(2)}, u32[]{:S(2)}) collective-permute-start(f32[4,64,128]{2,1,0:T(8,128)S(1)} %get-tuple-element.8), channel_id=1, source_target_pairs={{0,8},{8,0},{16,24},{24,16},{32,40},{40,32},{48,56},{56,48},{64,72... | collective-permute-start | bytes 393224 | tf_op jit(solution)/shard_map/ppermute | solution.py:217
  8.8 1.0 %collective-permute-done = f32[4,64,128]{2,1,0:T(8,128)S(1)} collective-permute-done((f32[4,64,128]{2,1,0:T(8,128)S(1)}, f32[4,64,128]{2,1,0:T(8,128)S(1)}, u32[]{:S(2)}, u32[]{:S(2)}) %collective-permute-start) | collective-permute-done | bytes 131104 | tf_op jit(solution)/shard_map/ppermute | solution.py:217
  9.8 1.3 %collective-permute-start.1 = (f32[64,128]{1,0:T(8,128)S(1)}, f32[64,128]{1,0:T(8,128)S(1)}, u32[]{:S(2)}, u32[]{:S(2)}) collective-permute-start(f32[64,128]{1,0:T(8,128)S(1)} %get-tuple-element.9), channel_id=1, source_target_pairs={{0,32},{8,40},{16,48},{24,56},{32,0},{40,8},{48,16},{56,24},{64,96... | collective-permute-start | bytes 98312 | tf_op jit(solution)/shard_map/ppermute | solution.py:220
  11.1 0.8 %collective-permute-start.3 = (f32[64,128]{1,0:T(8,128)S(1)}, f32[64,128]{1,0:T(8,128)S(1)}, u32[]{:S(2)}, u32[]{:S(2)}) collective-permute-start(f32[64,128]{1,0:T(8,128)S(1)} %get-tuple-element.10), channel_id=1, source_target_pairs={{0,48},{8,56},{16,0},{24,8},{32,16},{40,24},{48,32},{56,40},{64,11... | collective-permute-start | bytes 98312 | tf_op jit(solution)/shard_map/ppermute | solution.py:220
  11.9 0.7 %collective-permute-start.2 = (f32[64,128]{1,0:T(8,128)S(1)}, f32[64,128]{1,0:T(8,128)S(1)}, u32[]{:S(2)}, u32[]{:S(2)}) collective-permute-start(f32[64,128]{1,0:T(8,128)S(1)} %get-tuple-element.11), channel_id=1, source_target_pairs={{0,16},{8,24},{16,32},{24,40},{32,48},{40,56},{48,0},{56,8},{64,80... | collective-permute-start | bytes 98312 | tf_op jit(solution)/shard_map/ppermute | solution.py:220
  12.6 1.6 %collective-permute-done.1 = f32[64,128]{1,0:T(8,128)S(1)} collective-permute-done((f32[64,128]{1,0:T(8,128)S(1)}, f32[64,128]{1,0:T(8,128)S(1)}, u32[]{:S(2)}, u32[]{:S(2)}) %collective-permute-start.1) | collective-permute-done | bytes 32800 | tf_op jit(solution)/shard_map/ppermute | solution.py:220
  14.2 0.1 collective-permute-done.3
  14.3 1.6 %collective-permute-done.2 = f32[64,128]{1,0:T(8,128)S(1)} collective-permute-done((f32[64,128]{1,0:T(8,128)S(1)}, f32[64,128]{1,0:T(8,128)S(1)}, u32[]{:S(2)}, u32[]{:S(2)}) %collective-permute-start.2) | collective-permute-done | bytes 32800 | tf_op jit(solution)/shard_map/ppermute | solution.py:220
  15.9 6.1 %collective-permute-start.6 = (f32[64,128]{1,0:T(8,128)S(1)}, f32[64,128]{1,0:T(8,128)S(1)}, u32[]{:S(2)}, u32[]{:S(2)}) collective-permute-start(f32[64,128]{1,0:T(8,128)S(1)} %fusion.2.ref_0), channel_id=1, source_target_pairs={{0,192},{8,200},{16,208},{24,216},{32,224},{40,232},{48,240},{56,2... | collective-permute-start | bytes 98312 | tf_op jit(solution)/shard_map/ppermute | solution.py:222
  22.0 0.0 collective-permute-start.5
  22.0 3.3 %collective-permute-start.4 = (f32[64,128]{1,0:T(8,128)S(1)}, f32[64,128]{1,0:T(8,128)S(1)}, u32[]{:S(2)}, u32[]{:S(2)}) collective-permute-start(f32[64,128]{1,0:T(8,128)S(1)} %fusion.2.ref_0), channel_id=1, source_target_pairs={{0,128},{8,136},{16,144},{24,152},{32,160},{40,168},{48,176},{56,1... | collective-permute-start | bytes 98312 | tf_op jit(solution)/shard_map/ppermute | solution.py:222
  25.2 0.0 collective-permute-done.6.ref_3
  25.2 1.6 %collective-permute-done.5.ref_2 = f32[64,128]{1,0:T(8,128)S(1)} collective-permute-done((f32[64,128]{1,0:T(8,128)S(1)}, f32[64,128]{1,0:T(8,128)S(1)}, u32[]{:S(2)}, u32[]{:S(2)}) %collective-permute-start.5) | collective-permute-done | bytes 32800 | tf_op jit(solution)/shard_map/ppermute | solution.py:222
  26.8 1.8 %collective-permute-done.4.ref_1 = f32[64,128]{1,0:T(8,128)S(1)} collective-permute-done((f32[64,128]{1,0:T(8,128)S(1)}, f32[64,128]{1,0:T(8,128)S(1)}, u32[]{:S(2)}, u32[]{:S(2)}) %collective-permute-start.4) | collective-permute-done | bytes 32800 | tf_op jit(solution)/shard_map/ppermute | solution.py:222
  28.7 12.8 %all_to_all.5 = f32[32,3,4,128]{3,2,1,0:T(4,128)S(1)} all-to-all(f32[32,3,4,128]{3,2,1,0:T(4,128)S(1)} %bitcast.18), channel_id=1, replica_groups={{0,1,2,3,4,5,6,7,16,17,18,19,20,21,22,23,32,33,34,35,36,37,38,39,48,49,..., dimensions={0} | all-to-all | bytes 393216 | tf_op jit(solution)/shard_map/all_to_all | solution.py:227
  41.5 4.6 %collective-permute-start.7 = (f32[384,128]{1,0:T(8,128)S(1)}, f32[384,128]{1,0:T(8,128)S(1)}, u32[]{:S(2)}, u32[]{:S(2)}) collective-permute-start(f32[384,128]{1,0:T(8,128)S(1)} %bitcast.16), channel_id=1, source_target_pairs={{0,8},{8,0},{16,24},{24,16},{32,40},{40,32},{48,56},{56,48},{64,72... | collective-permute-start | bytes 589832 | tf_op jit(solution)/shard_map/ppermute | solution.py:229
  46.0 0.0 copy-done
  46.0 0.3 shard_map.57.earlier_ref
  46.4 0.7 %collective-permute-done.7.ref = f32[384,128]{1,0:T(8,128)S(1)} collective-permute-done((f32[384,128]{1,0:T(8,128)S(1)}, f32[384,128]{1,0:T(8,128)S(1)}, u32[]{:S(2)}, u32[]{:S(2)}) %collective-permute-start.7) | collective-permute-done | bytes 196640 | tf_op jit(solution)/shard_map/ppermute | solution.py:229
  47.1 1.3 %shard_map.58 = f32[256,1024]{1,0:T(8,128)} custom-call(f32[384,128]{1,0:T(8,128)S(1)} %collective-permute-done.7.ref, f32[256,1024]{1,0:T(8,128)S(1)} %shard_map.57.earlier_ref), custom_call_target="tpu_custom_call" | custom-call | flops 100663296 | bytes 1048576 | tf_op jit(solution)/shard_map/pallas_call | solution.py:201
  (4 shorter events, 0.1 us)
Async XLA Ops:
  0.0 46.0 %copy-start = (f32[256,1024]{1,0:T(8,128)S(1)}, f32[256,1024]{1,0:T(8,128)}, u32[]{:S(2)}) copy-start(f32[256,1024]{1,0:T(8,128)} %earlier_ref.1) | copy-start | bytes 3145732
  5.5 4.3 %collective-permute-start = (f32[4,64,128]{2,1,0:T(8,128)S(1)}, f32[4,64,128]{2,1,0:T(8,128)S(1)}, u32[]{:S(2)}, u32[]{:S(2)}) collective-permute-start(f32[4,64,128]{2,1,0:T(8,128)S(1)} %get-tuple-element.8), channel_id=1, source_target_pairs={{0,8},{8,0},{16,24},{24,16},{32,40},{40,32},{48,56},{56,48},{64,72... | collective-permute-start | bytes 393224 | tf_op jit(solution)/shard_map/ppermute | solution.py:217
  9.8 4.4 %collective-permute-start.1 = (f32[64,128]{1,0:T(8,128)S(1)}, f32[64,128]{1,0:T(8,128)S(1)}, u32[]{:S(2)}, u32[]{:S(2)}) collective-permute-start(f32[64,128]{1,0:T(8,128)S(1)} %get-tuple-element.9), channel_id=1, source_target_pairs={{0,32},{8,40},{16,48},{24,56},{32,0},{40,8},{48,16},{56,24},{64,96... | collective-permute-start | bytes 98312 | tf_op jit(solution)/shard_map/ppermute | solution.py:220
  11.1 3.2 %collective-permute-start.3 = (f32[64,128]{1,0:T(8,128)S(1)}, f32[64,128]{1,0:T(8,128)S(1)}, u32[]{:S(2)}, u32[]{:S(2)}) collective-permute-start(f32[64,128]{1,0:T(8,128)S(1)} %get-tuple-element.10), channel_id=1, source_target_pairs={{0,48},{8,56},{16,0},{24,8},{32,16},{40,24},{48,32},{56,40},{64,11... | collective-permute-start | bytes 98312 | tf_op jit(solution)/shard_map/ppermute | solution.py:220
  11.9 4.0 %collective-permute-start.2 = (f32[64,128]{1,0:T(8,128)S(1)}, f32[64,128]{1,0:T(8,128)S(1)}, u32[]{:S(2)}, u32[]{:S(2)}) collective-permute-start(f32[64,128]{1,0:T(8,128)S(1)} %get-tuple-element.11), channel_id=1, source_target_pairs={{0,16},{8,24},{16,32},{24,40},{32,48},{40,56},{48,0},{56,8},{64,80... | collective-permute-start | bytes 98312 | tf_op jit(solution)/shard_map/ppermute | solution.py:220
  15.9 9.4 %collective-permute-start.6 = (f32[64,128]{1,0:T(8,128)S(1)}, f32[64,128]{1,0:T(8,128)S(1)}, u32[]{:S(2)}, u32[]{:S(2)}) collective-permute-start(f32[64,128]{1,0:T(8,128)S(1)} %fusion.2.ref_0), channel_id=1, source_target_pairs={{0,192},{8,200},{16,208},{24,216},{32,224},{40,232},{48,240},{56,2... | collective-permute-start | bytes 98312 | tf_op jit(solution)/shard_map/ppermute | solution.py:222
  22.0 4.9 %collective-permute-start.5 = (f32[64,128]{1,0:T(8,128)S(1)}, f32[64,128]{1,0:T(8,128)S(1)}, u32[]{:S(2)}, u32[]{:S(2)}) collective-permute-start(f32[64,128]{1,0:T(8,128)S(1)} %fusion.2.ref_0), channel_id=1, source_target_pairs={{0,64},{8,72},{16,80},{24,88},{32,96},{40,104},{48,112},{56,120},{... | collective-permute-start | bytes 98312 | tf_op jit(solution)/shard_map/ppermute | solution.py:222
  22.0 6.7 %collective-permute-start.4 = (f32[64,128]{1,0:T(8,128)S(1)}, f32[64,128]{1,0:T(8,128)S(1)}, u32[]{:S(2)}, u32[]{:S(2)}) collective-permute-start(f32[64,128]{1,0:T(8,128)S(1)} %fusion.2.ref_0), channel_id=1, source_target_pairs={{0,128},{8,136},{16,144},{24,152},{32,160},{40,168},{48,176},{56,1... | collective-permute-start | bytes 98312 | tf_op jit(solution)/shard_map/ppermute | solution.py:222
  41.5 5.6 %collective-permute-start.7 = (f32[384,128]{1,0:T(8,128)S(1)}, f32[384,128]{1,0:T(8,128)S(1)}, u32[]{:S(2)}, u32[]{:S(2)}) collective-permute-start(f32[384,128]{1,0:T(8,128)S(1)} %bitcast.16), channel_id=1, source_target_pairs={{0,8},{8,0},{16,24},{24,16},{32,40},{40,32},{48,56},{56,48},{64,72... | collective-permute-start | bytes 589832 | tf_op jit(solution)/shard_map/ppermute | solution.py:229

commit v4 on v3

v4 whole, which is shorter than its diff:
```python
import functools

import jax
import jax.numpy as jnp
from jax import lax
from jax.experimental import pallas as pl
from jax.experimental.pallas import tpu as pltpu
from jax.sharding import PartitionSpec as P

PROJ = 2
LEN = 64
LANES = 128
BOTH = ("section", "dp")
ZH, Y, C, ZL, X = 4, 4, 2, 2, 4
SECTIONS, GROUPS = ZH * Y * C, ZL * X
PAIRS = SECTIONS // C
CHUNKS = (256, 768, 1024, 1024, 512, 512)
VMEM_BYTES = 24 * 2**20
F32 = jnp.float32


ACROSS_CORES = [(s, s ^ 1) for s in range(SECTIONS)]
def section_at(zh, y, c):
    return (zh * Y + y) * C + c


def across(by_zh, by_y):
    return [
        (section_at(zh, y, c), section_at(zh ^ by_zh, y ^ by_y, c))
        for zh in range(ZH)
        for y in range(Y)
        for c in range(C)
    ]


SAME_ZH = [
    [section_at(zh, y, c) * GROUPS + d for y in range(Y) for d in range(GROUPS)]
    for zh in range(ZH)
    for c in range(C)
]
SHARE = 3
OUT_PARTS = 2


def project(act, grad, weight_in, weight_out, first, size):
    at = slice(first, first + size)
    tokens = act.shape[0] * act.shape[1]
    k_out = weight_out.shape[1]
    return (
        jnp.dot(
            act[:, :, at].reshape(tokens, size),
            jnp.concatenate([weight_in[p, at, :] for p in range(PROJ)], axis=1),
            preferred_element_type=F32,
        ),
        lax.dot_general(
            grad[:, :, at].reshape(tokens, size),
            weight_out[:, :, at].reshape(PROJ * k_out, size),
            (((1,), (1,)), ((), ())),
            preferred_element_type=F32,
        ),
    )


def write_terms(sums, ref, term):
    y = lax.rem(lax.div(lax.axis_index("section"), C), Y)
    count, k_out, k_in = term.shape
    length = sums[0].shape[0] // count
    group = k_out // PAIRS
    low_in, low_out = (part.astype(jnp.bfloat16) for part in sums)
    for i in range(count):
        tokens = slice(i * length, (i + 1) * length)
        both = lax.dot_general(
            low_out[tokens],
            low_in[tokens],
            (((0,), (0,)), ((), ())),
            preferred_element_type=F32,
        )
        term[i] = both[:k_out, :k_in] + both[k_out:, k_in:]
        for k in range(group):
            ref[lax.bitwise_xor(y, k), pl.ds(i, PAIRS, stride=count), :] = term[
                i, pl.ds(k, PAIRS, stride=group), :
            ]


def theirs_kernel(
    act_ref, grad_ref, in_ref, out_ref,
    theirs_ref, act_mine, grad_mine, weight_in, weight_out,
    act, grad, term, sems, mine_sems,
):
    core = lax.rem(lax.axis_index("section"), C)
    half = act.shape[0]
    theirs, mine = pl.ds((1 - core) * half, half), pl.ds(core * half, half)
    spans = [(sum(CHUNKS[:c]), size) for c, size in enumerate(CHUNKS)]

    def copies(c):
        at = pl.ds(*spans[c])
        return [
            pltpu.make_async_copy(in_ref.at[0, :, at, :], weight_in.at[:, at, :], sems.at[c, 0]),
            pltpu.make_async_copy(act_ref.at[0, theirs, :, at], act.at[:, :, at], sems.at[c, 1]),
            pltpu.make_async_copy(out_ref.at[0, :, :, at], weight_out.at[:, :, at], sems.at[c, 2]),
            pltpu.make_async_copy(grad_ref.at[0, theirs, :, at], grad.at[:, :, at], sems.at[c, 3]),
        ]

    later = [
        pltpu.make_async_copy(act_ref.at[0, mine], act_mine, mine_sems.at[0]),
        pltpu.make_async_copy(grad_ref.at[0, mine], grad_mine, mine_sems.at[1]),
    ]
    for c in range(len(spans)):
        for copy in copies(c):
            copy.start()
    for copy in later:
        copy.start()
    sums = None
    for c in range(len(spans)):
        for copy in copies(c):
            copy.wait()
        parts = project(act, grad, weight_in, weight_out, *spans[c])
        sums = parts if sums is None else [s + p for s, p in zip(sums, parts)]
    write_terms(sums, theirs_ref, term)
    for copy in later:
        copy.wait()


def mine_kernel(act, grad, weight_in, weight_out, mine_ref, term):
    sums = None
    size = 1024
    for first in range(0, act.shape[2], size):
        parts = project(act, grad, weight_in, weight_out, first, size)
        sums = parts if sums is None else [s + p for s, p in zip(sums, parts)]
    write_terms(sums, mine_ref, term)


def layer_terms(activations, out_grads, proj_in, proj_out):
    count, length, width = activations.shape[1:]
    half = count // C
    k_in, k_out = proj_in.shape[3], proj_out.shape[2]
    piece = jax.ShapeDtypeStruct((k_out // PAIRS, PAIRS * half, k_in), F32)
    tokens = jax.ShapeDtypeStruct((half, length, width), jnp.bfloat16)
    vmem = pl.BlockSpec(memory_space=pltpu.VMEM)
    theirs, *kept = pl.pallas_call(
        theirs_kernel,
        in_specs=[pl.BlockSpec(memory_space=pl.ANY)] * 4,
        out_specs=[vmem] * 5,
        out_shape=[
            piece,
            tokens,
            tokens,
            jax.ShapeDtypeStruct(proj_in.shape[1:], jnp.bfloat16),
            jax.ShapeDtypeStruct(proj_out.shape[1:], jnp.bfloat16),
        ],
        scratch_shapes=[
            pltpu.VMEM(tokens.shape, jnp.bfloat16),
            pltpu.VMEM(tokens.shape, jnp.bfloat16),
            pltpu.VMEM((half, k_out, k_in), F32),
            pltpu.SemaphoreType.DMA((len(CHUNKS), 4)),
            pltpu.SemaphoreType.DMA((2,)),
        ],
        compiler_params=pltpu.CompilerParams(vmem_limit_bytes=VMEM_BYTES),
    )(*(pltpu.with_memory_space_constraint(a, pltpu.HBM) for a in (activations, out_grads, proj_in, proj_out)))
    mine = pl.pallas_call(
        mine_kernel,
        in_specs=[vmem] * 4,
        out_specs=vmem,
        out_shape=piece,
        scratch_shapes=[pltpu.VMEM((half, k_out, k_in), F32)],
        cost_estimate=pl.CostEstimate(
            flops=2 * half * length * width * PROJ * (k_in + k_out),
            bytes_accessed=8 * 2**20,
            transcendentals=0,
        ),
        compiler_params=pltpu.CompilerParams(vmem_limit_bytes=16 * 2**20),
    )(*kept)
    return mine, theirs


def thirds(value):
    parts = []
    for _ in range(3):
        part = value.astype(jnp.bfloat16)
        parts.append(part)
        value = value - part.astype(F32)
    return parts


def pack_kernel(ref_0, ref_1, ref_2, ref_3, packed_ref, reduced):
    zh = lax.div(lax.axis_index("section"), Y * C)
    reduced[...] = (ref_0[...] + ref_1[...]) + (ref_2[...] + ref_3[...])
    half = reduced.shape[0] // PAIRS
    for y in range(Y):
        row = reduced[pl.ds(pl.multiple_of((zh * Y + y) * half, half), half), :]
        for d in range(GROUPS):
            at = (y * GROUPS + d) * SHARE * half
            packed_ref[at : at + half, :] = row
            packed_ref[at + half : at + SHARE * half, :] = reduced[
                d * 2 * half : (d + 1) * 2 * half, :
            ]


def pack(pieces):
    shape = pieces[0].shape
    return pl.pallas_call(
        pack_kernel,
        in_specs=[pl.BlockSpec(memory_space=pltpu.VMEM)] * ZH,
        out_specs=pl.BlockSpec(memory_space=pltpu.VMEM),
        out_shape=jax.ShapeDtypeStruct(
            (Y * GROUPS * SHARE * (shape[0] // PAIRS), shape[1]), F32
        ),
        scratch_shapes=[pltpu.VMEM(shape, F32)],
        compiler_params=pltpu.CompilerParams(vmem_limit_bytes=8 * 2**20),
    )(*pieces)


def gathered(ref, k, row):
    half = ref.shape[0] // (Y * GROUPS * SHARE)
    return jnp.concatenate(
        [
            ref[pl.ds((k * GROUPS * SHARE + row) * half + e, GROUPS, stride=SHARE * half), :]
            for e in range(half)
        ],
        axis=0,
    )


def factors(ref, core, scale):
    r = thirds(
        jnp.concatenate([gathered(ref, core * 2 + k, 0) for k in range(2)], axis=1) * scale
    )
    c = thirds(
        jnp.concatenate([gathered(ref, k, 1 + j) for j in range(2) for k in range(4)], axis=1)
    )
    pairs = [(0, 0), (0, 1), (1, 0), (1, 1), (0, 2), (2, 0)]
    return (
        jnp.concatenate([r[i] for i, _ in pairs], axis=0),
        jnp.concatenate([c[j] for _, j in pairs], axis=0),
    )


def outer_product(ref, core, scale):
    rows, cols = factors(ref, core, scale)
    return lax.dot_general(
        rows, cols, (((0,), (0,)), ((), ())), preferred_element_type=F32
    )


def near_kernel(scale, ref, earlier_ref, held_ref):
    core = lax.rem(lax.axis_index("section"), C)
    held_ref[...] = earlier_ref[...] + outer_product(ref, core, scale)


def far_kernel(scale, ref, held_ref, gram_ref, total, sems):
    core = lax.rem(lax.axis_index("section"), C)
    rows, cols = factors(ref, core, scale)
    count = sems.shape[0]
    size = total.shape[0] // count
    copies = []
    for i in range(count):
        at = slice(i * size, (i + 1) * size)
        total[at, :] = held_ref[at, :] + lax.dot_general(
            rows[:, at], cols, (((0,), (0,)), ((), ())), preferred_element_type=F32
        )
        copy = pltpu.make_async_copy(total.at[at, :], gram_ref.at[at, :], sems.at[i])
        copy.start()
        copies.append(copy)
    for copy in copies:
        copy.wait()


def add_near(scale, features, earlier_gram):
    shape = earlier_gram.shape
    return pl.pallas_call(
        functools.partial(near_kernel, scale),
        in_specs=[pl.BlockSpec(memory_space=pltpu.VMEM)] * 2,
        out_specs=pl.BlockSpec(memory_space=pltpu.VMEM),
        out_shape=jax.ShapeDtypeStruct(shape, F32),
        cost_estimate=pl.CostEstimate(
            flops=12 * shape[0] * shape[1] * 32,
            bytes_accessed=4 * shape[0] * shape[1],
            transcendentals=0,
        ),
        compiler_params=pltpu.CompilerParams(vmem_limit_bytes=16 * 2**20),
    )(features, earlier_gram)


def add_far(scale, features, held):
    return pl.pallas_call(
        functools.partial(far_kernel, scale),
        in_specs=[pl.BlockSpec(memory_space=pltpu.VMEM)] * 2,
        out_specs=pl.BlockSpec(memory_space=pl.ANY),
        out_shape=jax.ShapeDtypeStruct(held.shape, F32),
        scratch_shapes=[
            pltpu.VMEM(held.shape, F32),
            pltpu.SemaphoreType.DMA((OUT_PARTS,)),
        ],
        compiler_params=pltpu.CompilerParams(vmem_limit_bytes=16 * 2**20),
    )(features, held)


def per_device(activations, out_grads, proj_in, proj_out, earlier_gram):
    mine, theirs = layer_terms(activations, out_grads, proj_in, proj_out)
    mine = mine + lax.ppermute(theirs, "section", ACROSS_CORES)
    reduced = mine[0]
    for turn in (2, 1, 3):
        reduced = reduced + lax.ppermute(mine[turn], "section", across(0, turn))
    pieces = [reduced] + [
        lax.ppermute(reduced, "section", across(turn, 0)) for turn in (1, 3, 2)
    ]
    packed = pack(pieces)
    rows = packed.shape[0] // (Y * GROUPS * SHARE)
    packed = packed.reshape(Y * GROUPS, SHARE, rows, LANES)
    near = lax.all_to_all(packed, BOTH, 0, 0, axis_index_groups=SAME_ZH)
    near = near.reshape(-1, LANES)
    far = lax.ppermute(near, "section", ACROSS_CORES)
    total_examples = activations.shape[1] * GROUPS
    scale = 1.0 / (LEN * SECTIONS * PROJ * total_examples)
    return add_far(scale, far, add_near(scale, near, earlier_gram))


def solution(mesh):
    return jax.shard_map(
        per_device,
        mesh=mesh,
        in_specs=(
            P("section", "dp", None, None),
            P("section", "dp", None, None),
            P("section", None, None, None),
            P("section", None, None, None),
            P("section", "dp"),
        ),
        out_specs=P("section", "dp"),
        check_vma=False,
    )
```

time: 48.5 us -> 47.4 us (0.977)
  starting transfers between devices: 20 us -> 18.5 us
  waiting for transfers between devices: 8.41 us -> 6.93 us
  blocking collectives: 12.8 us -> 13.9 us
  Pallas kernels: 7.12 us -> 7.83 us
    ppermute x6, starting transfers between devices: 12.1 us -> 10.9 us  [the longest x3 8.18 us: per_device(): lax.ppermute(reduced, 'section', across(turn, 0))]
    all_to_all x1, blocking collectives: 12.8 us -> 13.9 us  [per_device(): near = lax.all_to_all(packed, BOTH, 0, 0, axis_index_groups=SAME_ZH)]
    ppermute x1, waiting for transfers between devices: 0.99 us -> 0.01 us  [per_device(): mine = mine + lax.ppermute(theirs, 'section', ACROSS_CORES)]
    pallas_call x3 -> x4, Pallas kernels: 7.1 us -> 7.81 us  [the longest x1 4.75 us: layer_terms(): pl.pallas_call(theirs_kernel, in_specs=[pl.BlockSpec(memory_space=pl.ANY)...]
    ppermute x6, waiting for transfers between devices: 6.7 us -> 6.2 us  [the longest x3 3.69 us: per_device(): lax.ppermute(reduced, 'section', across(turn, 0))]
  transfers between devices with their start and end apart: 8 -> 8, of which waited for: 7 -> 5; matrix products, arithmetic and copies ran while one was open for 0% -> 0% of each run, Pallas kernels for 1% -> 4%
where the time goes in v4:
time: 47.4 us; the launch traced here: 47.3 us
  starting transfers between devices  18.5 us (39%)
  blocking collectives  13.9 us (29%)
  Pallas kernels  7.83 us (17%)
  waiting for transfers between devices  6.93 us (15%)
    all_to_all x1, blocking collectives, per_device(): near = lax.all_to_all(packed, BOTH, 0, 0, axis_index_groups=SAME_ZH)  13.9 us
    ppermute x3, starting transfers between devices, per_device(): lax.ppermute(reduced, 'section', across(turn, 0))  8.18 us
    pallas_call x1, Pallas kernels, layer_terms(): pl.pallas_call(theirs_kernel, in_specs=[pl.BlockSpec(memory_space=pl.ANY)...  4.75 us
    ppermute x1, starting transfers between devices, per_device(): far = lax.ppermute(near, 'section', ACROSS_CORES)  4.29 us
    ppermute x3, waiting for transfers between devices, per_device(): lax.ppermute(reduced, 'section', across(turn, 0))  3.69 us
    ppermute x1, starting transfers between devices, per_device(): mine = mine + lax.ppermute(theirs, 'section', ACROSS_CORES)  3.33 us
    ppermute x3, starting transfers between devices, per_device(): reduced = reduced + lax.ppermute(mine[turn], 'section', across(0, turn))  2.74 us
    ppermute x3, waiting for transfers between devices, per_device(): reduced = reduced + lax.ppermute(mine[turn], 'section', across(0, turn))  2.51 us
  transfers between devices with their start and end apart: 8, of which 5 were waited for; matrix products, arithmetic and copies ran while one was open for 0% of the time, Pallas kernels for 4%

profile of v4, /device:TPU:1, one launch (start us, length us, event | category | flops | bytes accessed | tf_op | source)
XLA Modules:
  0.0 47.3 jit_solution(6279926932455487665)
XLA Ops:
  0.0 4.7 %shard_map.55 = (f32[4,64,128]{2,1,0:T(8,128)S(1)}, bf16[4,64,4096]{2,1,0:T(8,128)(2,1)S(1)}, bf16[4,64,4096]{2,1,0:T(8,128)(2,1)S(1)}, bf16[2,4096,128]{2,1,0:T(8,128)(2,1)S(1)}, bf16[2,64,4096]{2,1,0:T(8,128)(2,1)S(1)}) custom-call(bf16[1,8,64,4096]{3,2,1,0:T(8,128)(2,1)} %act_ref.1, bf16[1,8,64,4096]{3,2,1,0:T(8,128)(2,1)} %grad_ref.1, ...), custom_call_target="tpu_custom_call" | custom-call | tf_op jit(solution)/shard_map/pallas_call | solution.py:140
  4.8 3.3 %collective-permute-start = (f32[4,64,128]{2,1,0:T(8,128)S(1)}, f32[4,64,128]{2,1,0:T(8,128)S(1)}, u32[]{:S(2)}, u32[]{:S(2)}) collective-permute-start(f32[4,64,128]{2,1,0:T(8,128)S(1)} %get-tuple-element.14), channel_id=1, source_target_pairs={{0,8},{8,0},{16,24},{24,16},{32,40},{40,32},{48,56},{56,48},{64,72... | collective-permute-start | bytes 393224 | tf_op jit(solution)/shard_map/ppermute | solution.py:300
  8.1 1.5 %shard_map.56 = f32[4,64,128]{2,1,0:T(8,128)S(1)} custom-call(bf16[4,64,4096]{2,1,0:T(8,128)(2,1)S(1)} %get-tuple-element.10.act, bf16[4,64,4096]{2,1,0:T(8,128)(2,1)S(1)} %get-tuple-element.11.grad, bf16[2,4096,128]{2,1,0:T(8,128)(2,1)S(1)} %get-tuple-element.12.weight_in, bf16[2,64,4096]{2,1,0:T(8,128)(2,1)S(1)} %get-tuple-element.13.weight_out), custom_call_target="tpu_custom_call" | custom-call | flops 805306368 | bytes 8388608 | tf_op jit(solution)/shard_map/pallas_call | solution.py:160
  9.6 0.0 copy-start
  9.6 0.0 collective-permute-done
  9.6 1.3 %collective-permute-start.1 = (f32[64,128]{1,0:T(8,128)S(1)}, f32[64,128]{1,0:T(8,128)S(1)}, u32[]{:S(2)}, u32[]{:S(2)}) collective-permute-start(f32[64,128]{1,0:T(8,128)S(1)} %get-tuple-element.15), channel_id=1, source_target_pairs={{0,32},{8,40},{16,48},{24,56},{32,0},{40,8},{48,16},{56,24},{64,96... | collective-permute-start | bytes 98312 | tf_op jit(solution)/shard_map/ppermute | solution.py:303
  10.9 0.8 %collective-permute-start.3 = (f32[64,128]{1,0:T(8,128)S(1)}, f32[64,128]{1,0:T(8,128)S(1)}, u32[]{:S(2)}, u32[]{:S(2)}) collective-permute-start(f32[64,128]{1,0:T(8,128)S(1)} %get-tuple-element.16), channel_id=1, source_target_pairs={{0,48},{8,56},{16,32},{24,40},{32,16},{40,24},{48,0},{56,8},{64,11... | collective-permute-start | bytes 98312 | tf_op jit(solution)/shard_map/ppermute | solution.py:303
  11.7 0.7 %collective-permute-start.2 = (f32[64,128]{1,0:T(8,128)S(1)}, f32[64,128]{1,0:T(8,128)S(1)}, u32[]{:S(2)}, u32[]{:S(2)}) collective-permute-start(f32[64,128]{1,0:T(8,128)S(1)} %get-tuple-element.17), channel_id=1, source_target_pairs={{0,16},{8,24},{16,0},{24,8},{32,48},{40,56},{48,32},{56,40},{64,80... | collective-permute-start | bytes 98312 | tf_op jit(solution)/shard_map/ppermute | solution.py:303
  12.4 1.6 %collective-permute-done.1 = f32[64,128]{1,0:T(8,128)S(1)} collective-permute-done((f32[64,128]{1,0:T(8,128)S(1)}, f32[64,128]{1,0:T(8,128)S(1)}, u32[]{:S(2)}, u32[]{:S(2)}) %collective-permute-start.1) | collective-permute-done | bytes 32800 | tf_op jit(solution)/shard_map/ppermute | solution.py:303
  14.0 0.9 %collective-permute-done.3 = f32[64,128]{1,0:T(8,128)S(1)} collective-permute-done((f32[64,128]{1,0:T(8,128)S(1)}, f32[64,128]{1,0:T(8,128)S(1)}, u32[]{:S(2)}, u32[]{:S(2)}) %collective-permute-start.3) | collective-permute-done | bytes 32800 | tf_op jit(solution)/shard_map/ppermute | solution.py:303
  14.9 0.0 collective-permute-done.2
  14.9 7.0 %collective-permute-start.6 = (f32[64,128]{1,0:T(8,128)S(1)}, f32[64,128]{1,0:T(8,128)S(1)}, u32[]{:S(2)}, u32[]{:S(2)}) collective-permute-start(f32[64,128]{1,0:T(8,128)S(1)} %fusion.2.ref_0), channel_id=1, source_target_pairs={{0,128},{8,136},{16,144},{24,152},{32,160},{40,168},{48,176},{56,1... | collective-permute-start | bytes 98312 | tf_op jit(solution)/shard_map/ppermute | solution.py:305
  21.9 0.0 collective-permute-start.5
  21.9 1.2 %collective-permute-start.4 = (f32[64,128]{1,0:T(8,128)S(1)}, f32[64,128]{1,0:T(8,128)S(1)}, u32[]{:S(2)}, u32[]{:S(2)}) collective-permute-start(f32[64,128]{1,0:T(8,128)S(1)} %fusion.2.ref_0), channel_id=1, source_target_pairs={{0,64},{8,72},{16,80},{24,88},{32,96},{40,104},{48,112},{56,120},{... | collective-permute-start | bytes 98312 | tf_op jit(solution)/shard_map/ppermute | solution.py:305
  23.1 0.1 collective-permute-done.6.ref_3
  23.2 3.6 %collective-permute-done.5.ref_2 = f32[64,128]{1,0:T(8,128)S(1)} collective-permute-done((f32[64,128]{1,0:T(8,128)S(1)}, f32[64,128]{1,0:T(8,128)S(1)}, u32[]{:S(2)}, u32[]{:S(2)}) %collective-permute-start.5) | collective-permute-done | bytes 32800 | tf_op jit(solution)/shard_map/ppermute | solution.py:305
  26.7 0.0 collective-permute-done.4.ref_1
  26.8 13.9 %all_to_all.5 = f32[32,3,4,128]{3,2,1,0:T(4,128)S(1)} all-to-all(f32[32,3,4,128]{3,2,1,0:T(4,128)S(1)} %bitcast.18), channel_id=1, replica_groups={{0,1,2,3,4,5,6,7,16,17,18,19,20,21,22,23,32,33,34,35,36,37,38,39,48,49,..., dimensions={0} | all-to-all | bytes 393216 | tf_op jit(solution)/shard_map/all_to_all | solution.py:310
  40.7 4.3 %collective-permute-start.7 = (f32[384,128]{1,0:T(8,128)S(1)}, f32[384,128]{1,0:T(8,128)S(1)}, u32[]{:S(2)}, u32[]{:S(2)}) collective-permute-start(f32[384,128]{1,0:T(8,128)S(1)} %bitcast.16), channel_id=1, source_target_pairs={{0,8},{8,0},{16,24},{24,16},{32,40},{40,32},{48,56},{56,48},{64,72... | collective-permute-start | bytes 589832 | tf_op jit(solution)/shard_map/ppermute | solution.py:312
  45.0 0.0 copy-done
  45.0 0.3 shard_map.58.held_ref
  45.3 0.7 %collective-permute-done.7.ref = f32[384,128]{1,0:T(8,128)S(1)} collective-permute-done((f32[384,128]{1,0:T(8,128)S(1)}, f32[384,128]{1,0:T(8,128)S(1)}, u32[]{:S(2)}, u32[]{:S(2)}) %collective-permute-start.7) | collective-permute-done | bytes 196640 | tf_op jit(solution)/shard_map/ppermute | solution.py:312
  46.1 1.3 %shard_map.59 = f32[256,1024]{1,0:T(8,128)} custom-call(f32[384,128]{1,0:T(8,128)S(1)} %collective-permute-done.7.ref, f32[256,1024]{1,0:T(8,128)S(1)} %shard_map.58.held_ref), custom_call_target="tpu_custom_call" | custom-call | tf_op jit(solution)/shard_map/pallas_call | solution.py:285
  (4 shorter events, 0.1 us)
Async XLA Ops:
  4.8 4.8 %collective-permute-start = (f32[4,64,128]{2,1,0:T(8,128)S(1)}, f32[4,64,128]{2,1,0:T(8,128)S(1)}, u32[]{:S(2)}, u32[]{:S(2)}) collective-permute-start(f32[4,64,128]{2,1,0:T(8,128)S(1)} %get-tuple-element.14), channel_id=1, source_target_pairs={{0,8},{8,0},{16,24},{24,16},{32,40},{40,32},{48,56},{56,48},{64,72... | collective-permute-start | bytes 393224 | tf_op jit(solution)/shard_map/ppermute | solution.py:300
  9.6 35.4 %copy-start = (f32[256,1024]{1,0:T(8,128)S(1)}, f32[256,1024]{1,0:T(8,128)}, u32[]{:S(2)}) copy-start(f32[256,1024]{1,0:T(8,128)} %earlier_ref.1) | copy-start | bytes 3145732
  9.6 4.4 %collective-permute-start.1 = (f32[64,128]{1,0:T(8,128)S(1)}, f32[64,128]{1,0:T(8,128)S(1)}, u32[]{:S(2)}, u32[]{:S(2)}) collective-permute-start(f32[64,128]{1,0:T(8,128)S(1)} %get-tuple-element.15), channel_id=1, source_target_pairs={{0,32},{8,40},{16,48},{24,56},{32,0},{40,8},{48,16},{56,24},{64,96... | collective-permute-start | bytes 98312 | tf_op jit(solution)/shard_map/ppermute | solution.py:303
  10.9 4.0 %collective-permute-start.3 = (f32[64,128]{1,0:T(8,128)S(1)}, f32[64,128]{1,0:T(8,128)S(1)}, u32[]{:S(2)}, u32[]{:S(2)}) collective-permute-start(f32[64,128]{1,0:T(8,128)S(1)} %get-tuple-element.16), channel_id=1, source_target_pairs={{0,48},{8,56},{16,32},{24,40},{32,16},{40,24},{48,0},{56,8},{64,11... | collective-permute-start | bytes 98312 | tf_op jit(solution)/shard_map/ppermute | solution.py:303
  11.7 3.2 %collective-permute-start.2 = (f32[64,128]{1,0:T(8,128)S(1)}, f32[64,128]{1,0:T(8,128)S(1)}, u32[]{:S(2)}, u32[]{:S(2)}) collective-permute-start(f32[64,128]{1,0:T(8,128)S(1)} %get-tuple-element.17), channel_id=1, source_target_pairs={{0,16},{8,24},{16,0},{24,8},{32,48},{40,56},{48,32},{56,40},{64,80... | collective-permute-start | bytes 98312 | tf_op jit(solution)/shard_map/ppermute | solution.py:303
  14.9 8.3 %collective-permute-start.6 = (f32[64,128]{1,0:T(8,128)S(1)}, f32[64,128]{1,0:T(8,128)S(1)}, u32[]{:S(2)}, u32[]{:S(2)}) collective-permute-start(f32[64,128]{1,0:T(8,128)S(1)} %fusion.2.ref_0), channel_id=1, source_target_pairs={{0,128},{8,136},{16,144},{24,152},{32,160},{40,168},{48,176},{56,1... | collective-permute-start | bytes 98312 | tf_op jit(solution)/shard_map/ppermute | solution.py:305
  21.9 4.9 %collective-permute-start.5 = (f32[64,128]{1,0:T(8,128)S(1)}, f32[64,128]{1,0:T(8,128)S(1)}, u32[]{:S(2)}, u32[]{:S(2)}) collective-permute-start(f32[64,128]{1,0:T(8,128)S(1)} %fusion.2.ref_0), channel_id=1, source_target_pairs={{0,192},{8,200},{16,208},{24,216},{32,224},{40,232},{48,240},{56,2... | collective-permute-start | bytes 98312 | tf_op jit(solution)/shard_map/ppermute | solution.py:305
  21.9 4.9 %collective-permute-start.4 = (f32[64,128]{1,0:T(8,128)S(1)}, f32[64,128]{1,0:T(8,128)S(1)}, u32[]{:S(2)}, u32[]{:S(2)}) collective-permute-start(f32[64,128]{1,0:T(8,128)S(1)} %fusion.2.ref_0), channel_id=1, source_target_pairs={{0,64},{8,72},{16,80},{24,88},{32,96},{40,104},{48,112},{56,120},{... | collective-permute-start | bytes 98312 | tf_op jit(solution)/shard_map/ppermute | solution.py:305
  40.7 5.4 %collective-permute-start.7 = (f32[384,128]{1,0:T(8,128)S(1)}, f32[384,128]{1,0:T(8,128)S(1)}, u32[]{:S(2)}, u32[]{:S(2)}) collective-permute-start(f32[384,128]{1,0:T(8,128)S(1)} %bitcast.16), channel_id=1, source_target_pairs={{0,8},{8,0},{16,24},{24,16},{32,40},{40,32},{48,56},{56,48},{64,72... | collective-permute-start | bytes 589832 | tf_op jit(solution)/shard_map/ppermute | solution.py:312

commit v5 on v4

--- a/solution.py
+++ b/solution.py
@@ -34,7 +34,7 @@
 
 
 SAME_ZH = [
-    [section_at(zh, y, c) * GROUPS + d for y in range(Y) for d in range(GROUPS)]
+    [section_at(zh, y, c) * GROUPS + d for y in reversed(range(Y)) for d in reversed(range(GROUPS))]
     for zh in range(ZH)
     for c in range(C)
 ]
@@ -189,7 +189,7 @@
     for y in range(Y):
         row = reduced[pl.ds(pl.multiple_of((zh * Y + y) * half, half), half), :]
         for d in range(GROUPS):
-            at = (y * GROUPS + d) * SHARE * half
+            at = ((Y - 1 - y) * GROUPS + GROUPS - 1 - d) * SHARE * half
             packed_ref[at : at + half, :] = row
             packed_ref[at + half : at + SHARE * half, :] = reduced[
                 d * 2 * half : (d + 1) * 2 * half, :
@@ -214,7 +214,7 @@
     half = ref.shape[0] // (Y * GROUPS * SHARE)
     return jnp.concatenate(
         [
-            ref[pl.ds((k * GROUPS * SHARE + row) * half + e, GROUPS, stride=SHARE * half), :]
+            ref[pl.ds(((Y - 1 - k) * GROUPS * SHARE + row) * half + e, GROUPS, stride=SHARE * half), :]
             for e in range(half)
         ],
         axis=0,

time: 47.4 us -> 45.4 us (0.958)
  blocking collectives: 13.9 us -> 11.8 us
    all_to_all x1, blocking collectives: 13.9 us -> 11.8 us  [per_device(): near = lax.all_to_all(packed, BOTH, 0, 0, axis_index_groups=SAME_ZH)]
where the time goes in v5:
time: 45.4 us; the launch traced here: 45.3 us
  starting transfers between devices  18.6 us (41%)
  blocking collectives  11.8 us (26%)
  Pallas kernels  7.84 us (17%)
  waiting for transfers between devices  6.92 us (15%)
    all_to_all x1, blocking collectives, per_device(): near = lax.all_to_all(packed, BOTH, 0, 0, axis_index_groups=SAME_ZH)  11.8 us
    ppermute x3, starting transfers between devices, per_device(): lax.ppermute(reduced, 'section', across(turn, 0))  8.18 us
    pallas_call x1, Pallas kernels, layer_terms(): pl.pallas_call(theirs_kernel, in_specs=[pl.BlockSpec(memory_space=pl.ANY)...  4.75 us
    ppermute x1, starting transfers between devices, per_device(): far = lax.ppermute(near, 'section', ACROSS_CORES)  4.31 us
    ppermute x3, waiting for transfers between devices, per_device(): lax.ppermute(reduced, 'section', across(turn, 0))  3.69 us
    ppermute x1, starting transfers between devices, per_device(): mine = mine + lax.ppermute(theirs, 'section', ACROSS_CORES)  3.33 us
    ppermute x3, starting transfers between devices, per_device(): reduced = reduced + lax.ppermute(mine[turn], 'section', across(0, turn))  2.74 us
    ppermute x3, waiting for transfers between devices, per_device(): reduced = reduced + lax.ppermute(mine[turn], 'section', across(0, turn))  2.51 us
  transfers between devices with their start and end apart: 8, of which 5 were waited for; matrix products, arithmetic and copies ran while one was open for 0% of the time, Pallas kernels for 4%

profile of v5, /device:TPU:1, one launch (start us, length us, event | category | flops | bytes accessed | tf_op | source)
XLA Modules:
  0.0 45.3 jit_solution(769376783840554556)
XLA Ops:
  0.0 4.7 %shard_map.55 = (f32[4,64,128]{2,1,0:T(8,128)S(1)}, bf16[4,64,4096]{2,1,0:T(8,128)(2,1)S(1)}, bf16[4,64,4096]{2,1,0:T(8,128)(2,1)S(1)}, bf16[2,4096,128]{2,1,0:T(8,128)(2,1)S(1)}, bf16[2,64,4096]{2,1,0:T(8,128)(2,1)S(1)}) custom-call(bf16[1,8,64,4096]{3,2,1,0:T(8,128)(2,1)} %act_ref.1, bf16[1,8,64,4096]{3,2,1,0:T(8,128)(2,1)} %grad_ref.1, ...), custom_call_target="tpu_custom_call" | custom-call | tf_op jit(solution)/shard_map/pallas_call | solution.py:140
  4.8 3.3 %collective-permute-start = (f32[4,64,128]{2,1,0:T(8,128)S(1)}, f32[4,64,128]{2,1,0:T(8,128)S(1)}, u32[]{:S(2)}, u32[]{:S(2)}) collective-permute-start(f32[4,64,128]{2,1,0:T(8,128)S(1)} %get-tuple-element.14), channel_id=1, source_target_pairs={{0,8},{8,0},{16,24},{24,16},{32,40},{40,32},{48,56},{56,48},{64,72... | collective-permute-start | bytes 393224 | tf_op jit(solution)/shard_map/ppermute | solution.py:300
  8.1 1.5 %shard_map.56 = f32[4,64,128]{2,1,0:T(8,128)S(1)} custom-call(bf16[4,64,4096]{2,1,0:T(8,128)(2,1)S(1)} %get-tuple-element.10.act, bf16[4,64,4096]{2,1,0:T(8,128)(2,1)S(1)} %get-tuple-element.11.grad, bf16[2,4096,128]{2,1,0:T(8,128)(2,1)S(1)} %get-tuple-element.12.weight_in, bf16[2,64,4096]{2,1,0:T(8,128)(2,1)S(1)} %get-tuple-element.13.weight_out), custom_call_target="tpu_custom_call" | custom-call | flops 805306368 | bytes 8388608 | tf_op jit(solution)/shard_map/pallas_call | solution.py:160
  9.6 0.0 copy-start
  9.6 0.0 collective-permute-done
  9.6 1.3 %collective-permute-start.1 = (f32[64,128]{1,0:T(8,128)S(1)}, f32[64,128]{1,0:T(8,128)S(1)}, u32[]{:S(2)}, u32[]{:S(2)}) collective-permute-start(f32[64,128]{1,0:T(8,128)S(1)} %get-tuple-element.15), channel_id=1, source_target_pairs={{0,32},{8,40},{16,48},{24,56},{32,0},{40,8},{48,16},{56,24},{64,96... | collective-permute-start | bytes 98312 | tf_op jit(solution)/shard_map/ppermute | solution.py:303
  10.9 0.8 %collective-permute-start.3 = (f32[64,128]{1,0:T(8,128)S(1)}, f32[64,128]{1,0:T(8,128)S(1)}, u32[]{:S(2)}, u32[]{:S(2)}) collective-permute-start(f32[64,128]{1,0:T(8,128)S(1)} %get-tuple-element.16), channel_id=1, source_target_pairs={{0,48},{8,56},{16,32},{24,40},{32,16},{40,24},{48,0},{56,8},{64,11... | collective-permute-start | bytes 98312 | tf_op jit(solution)/shard_map/ppermute | solution.py:303
  11.7 0.7 %collective-permute-start.2 = (f32[64,128]{1,0:T(8,128)S(1)}, f32[64,128]{1,0:T(8,128)S(1)}, u32[]{:S(2)}, u32[]{:S(2)}) collective-permute-start(f32[64,128]{1,0:T(8,128)S(1)} %get-tuple-element.17), channel_id=1, source_target_pairs={{0,16},{8,24},{16,0},{24,8},{32,48},{40,56},{48,32},{56,40},{64,80... | collective-permute-start | bytes 98312 | tf_op jit(solution)/shard_map/ppermute | solution.py:303
  12.4 1.6 %collective-permute-done.1 = f32[64,128]{1,0:T(8,128)S(1)} collective-permute-done((f32[64,128]{1,0:T(8,128)S(1)}, f32[64,128]{1,0:T(8,128)S(1)}, u32[]{:S(2)}, u32[]{:S(2)}) %collective-permute-start.1) | collective-permute-done | bytes 32800 | tf_op jit(solution)/shard_map/ppermute | solution.py:303
  14.0 0.9 %collective-permute-done.3 = f32[64,128]{1,0:T(8,128)S(1)} collective-permute-done((f32[64,128]{1,0:T(8,128)S(1)}, f32[64,128]{1,0:T(8,128)S(1)}, u32[]{:S(2)}, u32[]{:S(2)}) %collective-permute-start.3) | collective-permute-done | bytes 32800 | tf_op jit(solution)/shard_map/ppermute | solution.py:303
  14.9 0.0 collective-permute-done.2
  14.9 7.0 %collective-permute-start.6 = (f32[64,128]{1,0:T(8,128)S(1)}, f32[64,128]{1,0:T(8,128)S(1)}, u32[]{:S(2)}, u32[]{:S(2)}) collective-permute-start(f32[64,128]{1,0:T(8,128)S(1)} %fusion.2.ref_0), channel_id=1, source_target_pairs={{0,128},{8,136},{16,144},{24,152},{32,160},{40,168},{48,176},{56,1... | collective-permute-start | bytes 98312 | tf_op jit(solution)/shard_map/ppermute | solution.py:305
  21.9 0.0 collective-permute-start.5
  21.9 1.2 %collective-permute-start.4 = (f32[64,128]{1,0:T(8,128)S(1)}, f32[64,128]{1,0:T(8,128)S(1)}, u32[]{:S(2)}, u32[]{:S(2)}) collective-permute-start(f32[64,128]{1,0:T(8,128)S(1)} %fusion.2.ref_0), channel_id=1, source_target_pairs={{0,64},{8,72},{16,80},{24,88},{32,96},{40,104},{48,112},{56,120},{... | collective-permute-start | bytes 98312 | tf_op jit(solution)/shard_map/ppermute | solution.py:305
  23.1 0.1 collective-permute-done.6.ref_3
  23.2 3.6 %collective-permute-done.5.ref_2 = f32[64,128]{1,0:T(8,128)S(1)} collective-permute-done((f32[64,128]{1,0:T(8,128)S(1)}, f32[64,128]{1,0:T(8,128)S(1)}, u32[]{:S(2)}, u32[]{:S(2)}) %collective-permute-start.5) | collective-permute-done | bytes 32800 | tf_op jit(solution)/shard_map/ppermute | solution.py:305
  26.7 0.0 collective-permute-done.4.ref_1
  26.8 11.8 %all_to_all.5 = f32[32,3,4,128]{3,2,1,0:T(4,128)S(1)} all-to-all(f32[32,3,4,128]{3,2,1,0:T(4,128)S(1)} %bitcast.18), channel_id=1, replica_groups={{55,54,53,52,51,50,49,48,39,38,37,36,35,34,33,32,23,22,21,20,19,18,17,1..., dimensions={0} | all-to-all | bytes 393216 | tf_op jit(solution)/shard_map/all_to_all | solution.py:310
  38.6 4.3 %collective-permute-start.7 = (f32[384,128]{1,0:T(8,128)S(1)}, f32[384,128]{1,0:T(8,128)S(1)}, u32[]{:S(2)}, u32[]{:S(2)}) collective-permute-start(f32[384,128]{1,0:T(8,128)S(1)} %bitcast.16), channel_id=1, source_target_pairs={{0,8},{8,0},{16,24},{24,16},{32,40},{40,32},{48,56},{56,48},{64,72... | collective-permute-start | bytes 589832 | tf_op jit(solution)/shard_map/ppermute | solution.py:312
  42.9 0.0 copy-done
  42.9 0.3 shard_map.58.held_ref
  43.3 0.7 %collective-permute-done.7.ref = f32[384,128]{1,0:T(8,128)S(1)} collective-permute-done((f32[384,128]{1,0:T(8,128)S(1)}, f32[384,128]{1,0:T(8,128)S(1)}, u32[]{:S(2)}, u32[]{:S(2)}) %collective-permute-start.7) | collective-permute-done | bytes 196640 | tf_op jit(solution)/shard_map/ppermute | solution.py:312
  44.0 1.3 %shard_map.59 = f32[256,1024]{1,0:T(8,128)} custom-call(f32[384,128]{1,0:T(8,128)S(1)} %collective-permute-done.7.ref, f32[256,1024]{1,0:T(8,128)S(1)} %shard_map.58.held_ref), custom_call_target="tpu_custom_call" | custom-call | tf_op jit(solution)/shard_map/pallas_call | solution.py:285
  (4 shorter events, 0.1 us)
Async XLA Ops:
  4.8 4.8 %collective-permute-start = (f32[4,64,128]{2,1,0:T(8,128)S(1)}, f32[4,64,128]{2,1,0:T(8,128)S(1)}, u32[]{:S(2)}, u32[]{:S(2)}) collective-permute-start(f32[4,64,128]{2,1,0:T(8,128)S(1)} %get-tuple-element.14), channel_id=1, source_target_pairs={{0,8},{8,0},{16,24},{24,16},{32,40},{40,32},{48,56},{56,48},{64,72... | collective-permute-start | bytes 393224 | tf_op jit(solution)/shard_map/ppermute | solution.py:300
  9.6 33.4 %copy-start = (f32[256,1024]{1,0:T(8,128)S(1)}, f32[256,1024]{1,0:T(8,128)}, u32[]{:S(2)}) copy-start(f32[256,1024]{1,0:T(8,128)} %earlier_ref.1) | copy-start | bytes 3145732
  9.6 4.4 %collective-permute-start.1 = (f32[64,128]{1,0:T(8,128)S(1)}, f32[64,128]{1,0:T(8,128)S(1)}, u32[]{:S(2)}, u32[]{:S(2)}) collective-permute-start(f32[64,128]{1,0:T(8,128)S(1)} %get-tuple-element.15), channel_id=1, source_target_pairs={{0,32},{8,40},{16,48},{24,56},{32,0},{40,8},{48,16},{56,24},{64,96... | collective-permute-start | bytes 98312 | tf_op jit(solution)/shard_map/ppermute | solution.py:303
  10.9 4.0 %collective-permute-start.3 = (f32[64,128]{1,0:T(8,128)S(1)}, f32[64,128]{1,0:T(8,128)S(1)}, u32[]{:S(2)}, u32[]{:S(2)}) collective-permute-start(f32[64,128]{1,0:T(8,128)S(1)} %get-tuple-element.16), channel_id=1, source_target_pairs={{0,48},{8,56},{16,32},{24,40},{32,16},{40,24},{48,0},{56,8},{64,11... | collective-permute-start | bytes 98312 | tf_op jit(solution)/shard_map/ppermute | solution.py:303
  11.7 3.2 %collective-permute-start.2 = (f32[64,128]{1,0:T(8,128)S(1)}, f32[64,128]{1,0:T(8,128)S(1)}, u32[]{:S(2)}, u32[]{:S(2)}) collective-permute-start(f32[64,128]{1,0:T(8,128)S(1)} %get-tuple-element.17), channel_id=1, source_target_pairs={{0,16},{8,24},{16,0},{24,8},{32,48},{40,56},{48,32},{56,40},{64,80... | collective-permute-start | bytes 98312 | tf_op jit(solution)/shard_map/ppermute | solution.py:303
  14.9 8.3 %collective-permute-start.6 = (f32[64,128]{1,0:T(8,128)S(1)}, f32[64,128]{1,0:T(8,128)S(1)}, u32[]{:S(2)}, u32[]{:S(2)}) collective-permute-start(f32[64,128]{1,0:T(8,128)S(1)} %fusion.2.ref_0), channel_id=1, source_target_pairs={{0,128},{8,136},{16,144},{24,152},{32,160},{40,168},{48,176},{56,1... | collective-permute-start | bytes 98312 | tf_op jit(solution)/shard_map/ppermute | solution.py:305
  21.9 4.9 %collective-permute-start.5 = (f32[64,128]{1,0:T(8,128)S(1)}, f32[64,128]{1,0:T(8,128)S(1)}, u32[]{:S(2)}, u32[]{:S(2)}) collective-permute-start(f32[64,128]{1,0:T(8,128)S(1)} %fusion.2.ref_0), channel_id=1, source_target_pairs={{0,192},{8,200},{16,208},{24,216},{32,224},{40,232},{48,240},{56,2... | collective-permute-start | bytes 98312 | tf_op jit(solution)/shard_map/ppermute | solution.py:305
  21.9 4.9 %collective-permute-start.4 = (f32[64,128]{1,0:T(8,128)S(1)}, f32[64,128]{1,0:T(8,128)S(1)}, u32[]{:S(2)}, u32[]{:S(2)}) collective-permute-start(f32[64,128]{1,0:T(8,128)S(1)} %fusion.2.ref_0), channel_id=1, source_target_pairs={{0,64},{8,72},{16,80},{24,88},{32,96},{40,104},{48,112},{56,120},{... | collective-permute-start | bytes 98312 | tf_op jit(solution)/shard_map/ppermute | solution.py:305
  38.6 5.4 %collective-permute-start.7 = (f32[384,128]{1,0:T(8,128)S(1)}, f32[384,128]{1,0:T(8,128)S(1)}, u32[]{:S(2)}, u32[]{:S(2)}) collective-permute-start(f32[384,128]{1,0:T(8,128)S(1)} %bitcast.16), channel_id=1, source_target_pairs={{0,8},{8,0},{16,24},{24,16},{32,40},{40,32},{48,56},{56,48},{64,72... | collective-permute-start | bytes 589832 | tf_op jit(solution)/shard_map/ppermute | solution.py:312

commit v6 on v5

--- a/solution.py
+++ b/solution.py
@@ -33,8 +33,10 @@
     ]
 
 
+Y_RANKS = (2, 3, 1, 0)
+D_RANKS = (7, 6, 5, 4, 3, 2, 1, 0)
 SAME_ZH = [
-    [section_at(zh, y, c) * GROUPS + d for y in reversed(range(Y)) for d in reversed(range(GROUPS))]
+    [section_at(zh, y, c) * GROUPS + d for y in Y_RANKS for d in D_RANKS]
     for zh in range(ZH)
     for c in range(C)
 ]
@@ -189,7 +191,7 @@
     for y in range(Y):
         row = reduced[pl.ds(pl.multiple_of((zh * Y + y) * half, half), half), :]
         for d in range(GROUPS):
-            at = ((Y - 1 - y) * GROUPS + GROUPS - 1 - d) * SHARE * half
+            at = (Y_RANKS.index(y) * GROUPS + D_RANKS.index(d)) * SHARE * half
             packed_ref[at : at + half, :] = row
             packed_ref[at + half : at + SHARE * half, :] = reduced[
                 d * 2 * half : (d + 1) * 2 * half, :
@@ -210,11 +212,17 @@
     )(*pieces)
 
 
+def y_rank(k):
+    if isinstance(k, int):
+        return Y_RANKS.index(k)
+    return sum(at * (k == y).astype(jnp.int32) for at, y in enumerate(Y_RANKS))
+
+
 def gathered(ref, k, row):
     half = ref.shape[0] // (Y * GROUPS * SHARE)
     return jnp.concatenate(
         [
-            ref[pl.ds(((Y - 1 - k) * GROUPS * SHARE + row) * half + e, GROUPS, stride=SHARE * half), :]
+            ref[pl.ds((y_rank(k) * GROUPS * SHARE + row) * half + e, GROUPS, stride=SHARE * half), :]
             for e in range(half)
         ],
         axis=0,

time: 45.4 us -> 45 us (level)
  no operation moved by 1% of the time
where the time goes in v6:
time: 45 us; the launch traced here: 44.8 us
  starting transfers between devices  18.6 us (41%)
  blocking collectives  11.4 us (25%)
  Pallas kernels  7.84 us (17%)
  waiting for transfers between devices  6.92 us (15%)
    all_to_all x1, blocking collectives, per_device(): near = lax.all_to_all(packed, BOTH, 0, 0, axis_index_groups=SAME_ZH)  11.4 us
    ppermute x3, starting transfers between devices, per_device(): lax.ppermute(reduced, 'section', across(turn, 0))  8.18 us
    pallas_call x1, Pallas kernels, layer_terms(): pl.pallas_call(theirs_kernel, in_specs=[pl.BlockSpec(memory_space=pl.ANY)...  4.75 us
    ppermute x1, starting transfers between devices, per_device(): far = lax.ppermute(near, 'section', ACROSS_CORES)  4.31 us
    ppermute x3, waiting for transfers between devices, per_device(): lax.ppermute(reduced, 'section', across(turn, 0))  3.69 us
    ppermute x1, starting transfers between devices, per_device(): mine = mine + lax.ppermute(theirs, 'section', ACROSS_CORES)  3.33 us
    ppermute x3, starting transfers between devices, per_device(): reduced = reduced + lax.ppermute(mine[turn], 'section', across(0, turn))  2.74 us
    ppermute x3, waiting for transfers between devices, per_device(): reduced = reduced + lax.ppermute(mine[turn], 'section', across(0, turn))  2.51 us
  transfers between devices with their start and end apart: 8, of which 5 were waited for; matrix products, arithmetic and copies ran while one was open for 0% of the time, Pallas kernels for 4%

profile of v6, /device:TPU:1, one launch (start us, length us, event | category | flops | bytes accessed | tf_op | source)
XLA Modules:
  0.0 44.8 jit_solution(4006532821384361347)
XLA Ops:
  0.0 4.7 %shard_map.55 = (f32[4,64,128]{2,1,0:T(8,128)S(1)}, bf16[4,64,4096]{2,1,0:T(8,128)(2,1)S(1)}, bf16[4,64,4096]{2,1,0:T(8,128)(2,1)S(1)}, bf16[2,4096,128]{2,1,0:T(8,128)(2,1)S(1)}, bf16[2,64,4096]{2,1,0:T(8,128)(2,1)S(1)}) custom-call(bf16[1,8,64,4096]{3,2,1,0:T(8,128)(2,1)} %act_ref.1, bf16[1,8,64,4096]{3,2,1,0:T(8,128)(2,1)} %grad_ref.1, ...), custom_call_target="tpu_custom_call" | custom-call | tf_op jit(solution)/shard_map/pallas_call | solution.py:142
  4.8 3.3 %collective-permute-start = (f32[4,64,128]{2,1,0:T(8,128)S(1)}, f32[4,64,128]{2,1,0:T(8,128)S(1)}, u32[]{:S(2)}, u32[]{:S(2)}) collective-permute-start(f32[4,64,128]{2,1,0:T(8,128)S(1)} %get-tuple-element.14), channel_id=1, source_target_pairs={{0,8},{8,0},{16,24},{24,16},{32,40},{40,32},{48,56},{56,48},{64,72... | collective-permute-start | bytes 393224 | tf_op jit(solution)/shard_map/ppermute | solution.py:308
  8.1 1.5 %shard_map.56 = f32[4,64,128]{2,1,0:T(8,128)S(1)} custom-call(bf16[4,64,4096]{2,1,0:T(8,128)(2,1)S(1)} %get-tuple-element.10.act, bf16[4,64,4096]{2,1,0:T(8,128)(2,1)S(1)} %get-tuple-element.11.grad, bf16[2,4096,128]{2,1,0:T(8,128)(2,1)S(1)} %get-tuple-element.12.weight_in, bf16[2,64,4096]{2,1,0:T(8,128)(2,1)S(1)} %get-tuple-element.13.weight_out), custom_call_target="tpu_custom_call" | custom-call | flops 805306368 | bytes 8388608 | tf_op jit(solution)/shard_map/pallas_call | solution.py:162
  9.6 0.0 copy-start
  9.6 0.0 collective-permute-done
  9.6 1.3 %collective-permute-start.1 = (f32[64,128]{1,0:T(8,128)S(1)}, f32[64,128]{1,0:T(8,128)S(1)}, u32[]{:S(2)}, u32[]{:S(2)}) collective-permute-start(f32[64,128]{1,0:T(8,128)S(1)} %get-tuple-element.15), channel_id=1, source_target_pairs={{0,32},{8,40},{16,48},{24,56},{32,0},{40,8},{48,16},{56,24},{64,96... | collective-permute-start | bytes 98312 | tf_op jit(solution)/shard_map/ppermute | solution.py:311
  10.9 0.8 %collective-permute-start.3 = (f32[64,128]{1,0:T(8,128)S(1)}, f32[64,128]{1,0:T(8,128)S(1)}, u32[]{:S(2)}, u32[]{:S(2)}) collective-permute-start(f32[64,128]{1,0:T(8,128)S(1)} %get-tuple-element.16), channel_id=1, source_target_pairs={{0,48},{8,56},{16,32},{24,40},{32,16},{40,24},{48,0},{56,8},{64,11... | collective-permute-start | bytes 98312 | tf_op jit(solution)/shard_map/ppermute | solution.py:311
  11.7 0.7 %collective-permute-start.2 = (f32[64,128]{1,0:T(8,128)S(1)}, f32[64,128]{1,0:T(8,128)S(1)}, u32[]{:S(2)}, u32[]{:S(2)}) collective-permute-start(f32[64,128]{1,0:T(8,128)S(1)} %get-tuple-element.17), channel_id=1, source_target_pairs={{0,16},{8,24},{16,0},{24,8},{32,48},{40,56},{48,32},{56,40},{64,80... | collective-permute-start | bytes 98312 | tf_op jit(solution)/shard_map/ppermute | solution.py:311
  12.4 1.6 %collective-permute-done.1 = f32[64,128]{1,0:T(8,128)S(1)} collective-permute-done((f32[64,128]{1,0:T(8,128)S(1)}, f32[64,128]{1,0:T(8,128)S(1)}, u32[]{:S(2)}, u32[]{:S(2)}) %collective-permute-start.1) | collective-permute-done | bytes 32800 | tf_op jit(solution)/shard_map/ppermute | solution.py:311
  14.0 0.9 %collective-permute-done.3 = f32[64,128]{1,0:T(8,128)S(1)} collective-permute-done((f32[64,128]{1,0:T(8,128)S(1)}, f32[64,128]{1,0:T(8,128)S(1)}, u32[]{:S(2)}, u32[]{:S(2)}) %collective-permute-start.3) | collective-permute-done | bytes 32800 | tf_op jit(solution)/shard_map/ppermute | solution.py:311
  14.9 0.0 collective-permute-done.2
  14.9 7.0 %collective-permute-start.6 = (f32[64,128]{1,0:T(8,128)S(1)}, f32[64,128]{1,0:T(8,128)S(1)}, u32[]{:S(2)}, u32[]{:S(2)}) collective-permute-start(f32[64,128]{1,0:T(8,128)S(1)} %fusion.2.ref_0), channel_id=1, source_target_pairs={{0,128},{8,136},{16,144},{24,152},{32,160},{40,168},{48,176},{56,1... | collective-permute-start | bytes 98312 | tf_op jit(solution)/shard_map/ppermute | solution.py:313
  21.9 0.0 collective-permute-start.5
  21.9 1.2 %collective-permute-start.4 = (f32[64,128]{1,0:T(8,128)S(1)}, f32[64,128]{1,0:T(8,128)S(1)}, u32[]{:S(2)}, u32[]{:S(2)}) collective-permute-start(f32[64,128]{1,0:T(8,128)S(1)} %fusion.2.ref_0), channel_id=1, source_target_pairs={{0,64},{8,72},{16,80},{24,88},{32,96},{40,104},{48,112},{56,120},{... | collective-permute-start | bytes 98312 | tf_op jit(solution)/shard_map/ppermute | solution.py:313
  23.1 0.1 collective-permute-done.6.ref_3
  23.2 3.6 %collective-permute-done.5.ref_2 = f32[64,128]{1,0:T(8,128)S(1)} collective-permute-done((f32[64,128]{1,0:T(8,128)S(1)}, f32[64,128]{1,0:T(8,128)S(1)}, u32[]{:S(2)}, u32[]{:S(2)}) %collective-permute-start.5) | collective-permute-done | bytes 32800 | tf_op jit(solution)/shard_map/ppermute | solution.py:313
  26.7 0.0 collective-permute-done.4.ref_1
  26.8 11.4 %all_to_all.5 = f32[32,3,4,128]{3,2,1,0:T(4,128)S(1)} all-to-all(f32[32,3,4,128]{3,2,1,0:T(4,128)S(1)} %bitcast.18), channel_id=1, replica_groups={{39,38,37,36,35,34,33,32,55,54,53,52,51,50,49,48,23,22,21,20,19,18,17,1..., dimensions={0} | all-to-all | bytes 393216 | tf_op jit(solution)/shard_map/all_to_all | solution.py:318
  38.2 4.3 %collective-permute-start.7 = (f32[384,128]{1,0:T(8,128)S(1)}, f32[384,128]{1,0:T(8,128)S(1)}, u32[]{:S(2)}, u32[]{:S(2)}) collective-permute-start(f32[384,128]{1,0:T(8,128)S(1)} %bitcast.16), channel_id=1, source_target_pairs={{0,8},{8,0},{16,24},{24,16},{32,40},{40,32},{48,56},{56,48},{64,72... | collective-permute-start | bytes 589832 | tf_op jit(solution)/shard_map/ppermute | solution.py:320
  42.5 0.0 copy-done
  42.5 0.3 shard_map.58.held_ref
  42.9 0.7 %collective-permute-done.7.ref = f32[384,128]{1,0:T(8,128)S(1)} collective-permute-done((f32[384,128]{1,0:T(8,128)S(1)}, f32[384,128]{1,0:T(8,128)S(1)}, u32[]{:S(2)}, u32[]{:S(2)}) %collective-permute-start.7) | collective-permute-done | bytes 196640 | tf_op jit(solution)/shard_map/ppermute | solution.py:320
  43.6 1.3 %shard_map.59 = f32[256,1024]{1,0:T(8,128)} custom-call(f32[384,128]{1,0:T(8,128)S(1)} %collective-permute-done.7.ref, f32[256,1024]{1,0:T(8,128)S(1)} %shard_map.58.held_ref), custom_call_target="tpu_custom_call" | custom-call | tf_op jit(solution)/shard_map/pallas_call | solution.py:293
  (4 shorter events, 0.1 us)
Async XLA Ops:
  4.8 4.8 %collective-permute-start = (f32[4,64,128]{2,1,0:T(8,128)S(1)}, f32[4,64,128]{2,1,0:T(8,128)S(1)}, u32[]{:S(2)}, u32[]{:S(2)}) collective-permute-start(f32[4,64,128]{2,1,0:T(8,128)S(1)} %get-tuple-element.14), channel_id=1, source_target_pairs={{0,8},{8,0},{16,24},{24,16},{32,40},{40,32},{48,56},{56,48},{64,72... | collective-permute-start | bytes 393224 | tf_op jit(solution)/shard_map/ppermute | solution.py:308
  9.6 33.0 %copy-start = (f32[256,1024]{1,0:T(8,128)S(1)}, f32[256,1024]{1,0:T(8,128)}, u32[]{:S(2)}) copy-start(f32[256,1024]{1,0:T(8,128)} %earlier_ref.1) | copy-start | bytes 3145732
  9.6 4.4 %collective-permute-start.1 = (f32[64,128]{1,0:T(8,128)S(1)}, f32[64,128]{1,0:T(8,128)S(1)}, u32[]{:S(2)}, u32[]{:S(2)}) collective-permute-start(f32[64,128]{1,0:T(8,128)S(1)} %get-tuple-element.15), channel_id=1, source_target_pairs={{0,32},{8,40},{16,48},{24,56},{32,0},{40,8},{48,16},{56,24},{64,96... | collective-permute-start | bytes 98312 | tf_op jit(solution)/shard_map/ppermute | solution.py:311
  10.9 4.0 %collective-permute-start.3 = (f32[64,128]{1,0:T(8,128)S(1)}, f32[64,128]{1,0:T(8,128)S(1)}, u32[]{:S(2)}, u32[]{:S(2)}) collective-permute-start(f32[64,128]{1,0:T(8,128)S(1)} %get-tuple-element.16), channel_id=1, source_target_pairs={{0,48},{8,56},{16,32},{24,40},{32,16},{40,24},{48,0},{56,8},{64,11... | collective-permute-start | bytes 98312 | tf_op jit(solution)/shard_map/ppermute | solution.py:311
  11.7 3.2 %collective-permute-start.2 = (f32[64,128]{1,0:T(8,128)S(1)}, f32[64,128]{1,0:T(8,128)S(1)}, u32[]{:S(2)}, u32[]{:S(2)}) collective-permute-start(f32[64,128]{1,0:T(8,128)S(1)} %get-tuple-element.17), channel_id=1, source_target_pairs={{0,16},{8,24},{16,0},{24,8},{32,48},{40,56},{48,32},{56,40},{64,80... | collective-permute-start | bytes 98312 | tf_op jit(solution)/shard_map/ppermute | solution.py:311
  14.9 8.3 %collective-permute-start.6 = (f32[64,128]{1,0:T(8,128)S(1)}, f32[64,128]{1,0:T(8,128)S(1)}, u32[]{:S(2)}, u32[]{:S(2)}) collective-permute-start(f32[64,128]{1,0:T(8,128)S(1)} %fusion.2.ref_0), channel_id=1, source_target_pairs={{0,128},{8,136},{16,144},{24,152},{32,160},{40,168},{48,176},{56,1... | collective-permute-start | bytes 98312 | tf_op jit(solution)/shard_map/ppermute | solution.py:313
  21.9 4.9 %collective-permute-start.5 = (f32[64,128]{1,0:T(8,128)S(1)}, f32[64,128]{1,0:T(8,128)S(1)}, u32[]{:S(2)}, u32[]{:S(2)}) collective-permute-start(f32[64,128]{1,0:T(8,128)S(1)} %fusion.2.ref_0), channel_id=1, source_target_pairs={{0,192},{8,200},{16,208},{24,216},{32,224},{40,232},{48,240},{56,2... | collective-permute-start | bytes 98312 | tf_op jit(solution)/shard_map/ppermute | solution.py:313
  21.9 4.9 %collective-permute-start.4 = (f32[64,128]{1,0:T(8,128)S(1)}, f32[64,128]{1,0:T(8,128)S(1)}, u32[]{:S(2)}, u32[]{:S(2)}) collective-permute-start(f32[64,128]{1,0:T(8,128)S(1)} %fusion.2.ref_0), channel_id=1, source_target_pairs={{0,64},{8,72},{16,80},{24,88},{32,96},{40,104},{48,112},{56,120},{... | collective-permute-start | bytes 98312 | tf_op jit(solution)/shard_map/ppermute | solution.py:313
  38.2 5.4 %collective-permute-start.7 = (f32[384,128]{1,0:T(8,128)S(1)}, f32[384,128]{1,0:T(8,128)S(1)}, u32[]{:S(2)}, u32[]{:S(2)}) collective-permute-start(f32[384,128]{1,0:T(8,128)S(1)} %bitcast.16), channel_id=1, source_target_pairs={{0,8},{8,0},{16,24},{24,16},{32,40},{40,32},{48,56},{56,48},{64,72... | collective-permute-start | bytes 589832 | tf_op jit(solution)/shard_map/ppermute | solution.py:320
